TPU v7x, 32 devices: a whole 2x2x4 slice. The times are simulated.
32 devices in a mesh: dp: 4 (over z), fsdp: 8 (over y, x, core).
Axes of the slice: x: 2, y: 2, z: 4, core: 2. Of those that a mesh axis runs over, the one named last changes fastest.
Arguments:
- x_in: bfloat16 [32768, 512], P(('dp', 'fsdp')), may hold values from -6 to 6
- y_in: float32 [32768, 512], P(('dp', 'fsdp')), may hold values from -6 to 6
- lengths: int32 [32, 16], P(('dp', 'fsdp')), may hold values from 0 to 1024, as said below
- w_qkv: bfloat16 [512, 1536], P(('dp', 'fsdp')), may hold values from -0.25 to 0.25
- w_out: bfloat16 [512, 512], P(('dp', 'fsdp')), may hold values from -1 to 1
- gain_one: bfloat16 [512], P(('dp', 'fsdp')), may hold values from 0.5 to 1.5
- bias_one: bfloat16 [512], P(('dp', 'fsdp')), may hold values from -0.5 to 0.5
- w_up: bfloat16 [512, 2048], P(('dp', 'fsdp')), may hold values from -0.25 to 0.25
- b_up: bfloat16 [2048], P(('dp', 'fsdp')), may hold values from -0.5 to 0.5
- w_down: bfloat16 [2048, 512], P(('dp', 'fsdp')), may hold values from -0.125 to 0.125
- gain_two: bfloat16 [512], P(('dp', 'fsdp')), may hold values from 0.5 to 1.5
- bias_two: bfloat16 [512], P(('dp', 'fsdp')), may hold values from -0.5 to 0.5
- grad_x: bfloat16 [32768, 512], P(('dp', 'fsdp')), may hold values from -6 to 6
- grad_y: bfloat16 [32768, 512], P(('dp', 'fsdp')), may hold values from -6 to 6
Outputs:
- x_out: bfloat16 [32768, 512], P(('dp', 'fsdp'))
- y_out: float32 [32768, 512], P(('dp', 'fsdp'))
- d_x: float32 [32768, 512], P(('dp', 'fsdp'))
- d_qkv: float32 [512, 1536], P(('dp', 'fsdp'))
- d_out: float32 [512, 512], P(('dp', 'fsdp'))
- d_gain_one: float32 [512], P(('dp', 'fsdp'))
- d_bias_one: float32 [512], P(('dp', 'fsdp'))
- d_up: float32 [512, 2048], P(('dp', 'fsdp'))
- d_b_up: float32 [2048], P(('dp', 'fsdp'))
- d_down: float32 [2048, 512], P(('dp', 'fsdp'))
- d_gain_two: float32 [512], P(('dp', 'fsdp'))
- d_bias_two: float32 [512], P(('dp', 'fsdp'))
Inputs may be any that keep to these rules, and one draw needn't show every extreme that they name: `lengths`: row g lists the sequences of slot group g in slot order; the first entry is positive, zeros are unused entries, each row sums to at most 1024, and in every draw some row holds a single sequence of exactly 1024 tokens.
All inputs are finite; a program needn't handle non-finite values.
Results may differ from a plain program's by a relative error of at most 0.012.
Values may be sent and summed in bfloat16 or wider, within the bound.
A program may use at most 192 MiB of HBM per device.

v0:
```python
import jax
import jax.numpy as jnp
from jax import lax
from jax.sharding import PartitionSpec as P

H = 8


EPSILON = 1e-05
NEGATIVE = -1e30


def layer_norm(summed, gain_vec, bias_vec):
    average = jnp.mean(summed, axis=-1, keepdims=True)
    centred = summed - average
    spread = jnp.mean(centred * centred, axis=-1, keepdims=True)
    return centred * lax.rsqrt(spread + EPSILON) * gain_vec + bias_vec


def gelu_tanh(values):
    return jax.nn.gelu(values, approximate=True)


def slot_layout(lengths_row, slots):
    bounds = jnp.cumsum(lengths_row)
    position = jnp.arange(slots, dtype=jnp.int32)
    segment = jnp.sum((bounds[None, :] <= position[:, None]).astype(jnp.int32), axis=1)
    active = position < bounds[-1]
    segment = jnp.where(active, segment, -1 - position)
    return (position, segment, active.astype(jnp.float32)[:, None])


def block_scores(queries, keys_all, position, segment, start, block_rows, factor):
    query_block = queries[start : start + block_rows]
    raw = (
        jnp.einsum("qhd,khd->hqk", query_block, keys_all, preferred_element_type=jnp.float32)
        * factor
    )
    allowed = (segment[start : start + block_rows, None] == segment[None, :]) & (
        position[None, :] <= position[start : start + block_rows, None]
    )
    return (query_block, jnp.where(allowed[None], raw, NEGATIVE))


def on_device(
    x_in,
    y_in,
    lengths,
    w_qkv,
    w_out,
    gain_one,
    bias_one,
    w_up,
    b_up,
    w_down,
    gain_two,
    bias_two,
    grad_x,
    grad_y,
):
    slots = x_in.shape[0]
    width = x_in.shape[1]
    head_size = width // H
    factor = head_size ** (-0.5)
    block_rows = min(512, slots)
    position, segment, active = slot_layout(lengths[0], slots)
    attn_kept = (
        lax.all_gather(w_qkv, ("dp", "fsdp"), axis=0, tiled=True),
        lax.all_gather(w_out, ("dp", "fsdp"), axis=0, tiled=True),
        lax.all_gather(gain_one, ("dp", "fsdp"), axis=0, tiled=True),
        lax.all_gather(bias_one, ("dp", "fsdp"), axis=0, tiled=True),
    )
    qkv_full, out_full, gain_first, bias_first = attn_kept
    qkv = jnp.dot(x_in, qkv_full, preferred_element_type=jnp.float32).astype(jnp.bfloat16)
    queries = qkv[:, :width].reshape(slots, H, head_size)
    keys_all = qkv[:, width : 2 * width].reshape(slots, H, head_size)
    values_all = qkv[:, 2 * width :].reshape(slots, H, head_size)
    pieces = []
    maxima = []
    totals = []
    for start in range(0, slots, block_rows):
        query_block, scores = block_scores(
            queries, keys_all, position, segment, start, block_rows, factor
        )
        row_max = jnp.max(scores, axis=-1, keepdims=True)
        expd = jnp.exp(scores - row_max)
        row_sum = jnp.sum(expd, axis=-1, keepdims=True)
        probs = (expd / row_sum).astype(jnp.bfloat16)
        pieces.append(
            jnp.einsum("hqk,khd->qhd", probs, values_all, preferred_element_type=jnp.float32)
        )
        maxima.append(row_max)
        totals.append(row_sum)
    attended = jnp.concatenate(pieces, axis=0).reshape(slots, width).astype(jnp.bfloat16)
    branch_a = jnp.dot(attended, out_full, preferred_element_type=jnp.float32)
    first_sum = x_in.astype(jnp.float32) + branch_a
    gain_first32 = gain_first.astype(jnp.float32)
    bias_first32 = bias_first.astype(jnp.float32)
    x_mid = layer_norm(first_sum, gain_first32, bias_first32)
    y_mid = y_in + branch_a
    ffn_kept = (
        lax.all_gather(w_up, ("dp", "fsdp"), axis=0, tiled=True),
        lax.all_gather(b_up, ("dp", "fsdp"), axis=0, tiled=True),
        lax.all_gather(w_down, ("dp", "fsdp"), axis=0, tiled=True),
        lax.all_gather(gain_two, ("dp", "fsdp"), axis=0, tiled=True),
        lax.all_gather(bias_two, ("dp", "fsdp"), axis=0, tiled=True),
    )
    up_full, up_bias, down_full, gain_second, bias_second = ffn_kept
    x_low = x_mid.astype(jnp.bfloat16)
    upper = jnp.dot(x_low, up_full, preferred_element_type=jnp.float32) + up_bias.astype(
        jnp.float32
    )
    hidden = gelu_tanh(upper).astype(jnp.bfloat16)
    branch_f = jnp.dot(hidden, down_full, preferred_element_type=jnp.float32)
    second_sum = x_mid + branch_f
    gain_second32 = gain_second.astype(jnp.float32)
    bias_second32 = bias_second.astype(jnp.float32)
    x_next = layer_norm(second_sum, gain_second32, bias_second32)
    x_out = (x_next * active).astype(jnp.bfloat16)
    y_out = (y_mid + branch_f) * active
    grad_xo = grad_x.astype(jnp.float32) * active
    grad_yo = grad_y.astype(jnp.float32) * active
    ffn_set = (
        lax.all_gather(w_up, ("dp", "fsdp"), axis=0, tiled=True),
        lax.all_gather(b_up, ("dp", "fsdp"), axis=0, tiled=True),
        lax.all_gather(w_down, ("dp", "fsdp"), axis=0, tiled=True),
        lax.all_gather(gain_two, ("dp", "fsdp"), axis=0, tiled=True),
        lax.all_gather(bias_two, ("dp", "fsdp"), axis=0, tiled=True),
    )
    up_back, unused_bias, down_back, unused_gain, unused_shift = ffn_set
    unused_value, second_back = jax.vjp(layer_norm, second_sum, gain_second32, bias_second32)
    grad_second, grad_gain_two, grad_bias_two = second_back(grad_xo)
    grad_branch_f = (grad_second + grad_yo).astype(jnp.bfloat16)
    grad_down = jnp.einsum("tf,td->fd", hidden, grad_branch_f, preferred_element_type=jnp.float32)
    grad_hidden = jnp.einsum(
        "td,fd->tf", grad_branch_f, down_back, preferred_element_type=jnp.float32
    )
    unused_upper, gelu_back = jax.vjp(gelu_tanh, upper)
    grad_upper = gelu_back(grad_hidden)[0].astype(jnp.bfloat16)
    grad_up_bias = jnp.sum(grad_upper.astype(jnp.float32), axis=0)
    grad_up = jnp.einsum("td,tf->df", x_low, grad_upper, preferred_element_type=jnp.float32)
    grad_mid = grad_second + jnp.einsum(
        "tf,df->td", grad_upper, up_back, preferred_element_type=jnp.float32
    )
    ffn_summed = (
        lax.psum_scatter(grad_up, ("dp", "fsdp"), scatter_dimension=0, tiled=True),
        lax.psum_scatter(grad_up_bias, ("dp", "fsdp"), scatter_dimension=0, tiled=True),
        lax.psum_scatter(grad_down, ("dp", "fsdp"), scatter_dimension=0, tiled=True),
        lax.psum_scatter(grad_gain_two, ("dp", "fsdp"), scatter_dimension=0, tiled=True),
        lax.psum_scatter(grad_bias_two, ("dp", "fsdp"), scatter_dimension=0, tiled=True),
    )
    attn_set = (
        lax.all_gather(w_qkv, ("dp", "fsdp"), axis=0, tiled=True),
        lax.all_gather(w_out, ("dp", "fsdp"), axis=0, tiled=True),
        lax.all_gather(gain_one, ("dp", "fsdp"), axis=0, tiled=True),
        lax.all_gather(bias_one, ("dp", "fsdp"), axis=0, tiled=True),
    )
    qkv_back, out_back, unused_gain_one, unused_bias_one = attn_set
    unused_norm, first_back = jax.vjp(layer_norm, first_sum, gain_first32, bias_first32)
    grad_first, grad_gain_one, grad_bias_one = first_back(grad_mid)
    grad_branch_a = (grad_first + grad_yo).astype(jnp.bfloat16)
    grad_out = jnp.einsum("tc,td->cd", attended, grad_branch_a, preferred_element_type=jnp.float32)
    grad_attended = jnp.einsum(
        "td,cd->tc", grad_branch_a, out_back, preferred_element_type=jnp.float32
    )
    grad_attended = grad_attended.astype(jnp.bfloat16).reshape(slots, H, head_size)
    grad_keys = jnp.zeros((slots, H, head_size), jnp.float32)
    grad_values = jnp.zeros((slots, H, head_size), jnp.float32)
    query_grads = []
    for number, start in enumerate(range(0, slots, block_rows)):
        query_block, scores = block_scores(
            queries, keys_all, position, segment, start, block_rows, factor
        )
        probs = jnp.exp(scores - maxima[number]) / totals[number]
        probs_low = probs.astype(jnp.bfloat16)
        grad_block = grad_attended[start : start + block_rows]
        grad_values = grad_values + jnp.einsum(
            "hqk,qhd->khd", probs_low, grad_block, preferred_element_type=jnp.float32
        )
        grad_probs = jnp.einsum(
            "qhd,khd->hqk", grad_block, values_all, preferred_element_type=jnp.float32
        )
        grad_scores = probs * (grad_probs - jnp.sum(probs * grad_probs, axis=-1, keepdims=True))
        grad_scores = grad_scores.astype(jnp.bfloat16)
        query_grads.append(
            jnp.einsum("hqk,khd->qhd", grad_scores, keys_all, preferred_element_type=jnp.float32)
            * factor
        )
        grad_keys = (
            grad_keys
            + jnp.einsum(
                "hqk,qhd->khd", grad_scores, query_block, preferred_element_type=jnp.float32
            )
            * factor
        )
    grad_qkv = jnp.concatenate(
        [
            jnp.concatenate(query_grads, axis=0).reshape(slots, width),
            grad_keys.reshape(slots, width),
            grad_values.reshape(slots, width),
        ],
        axis=1,
    ).astype(jnp.bfloat16)
    grad_proj = jnp.einsum("tc,te->ce", x_in, grad_qkv, preferred_element_type=jnp.float32)
    grad_input = (
        jnp.einsum("te,ce->tc", grad_qkv, qkv_back, preferred_element_type=jnp.float32) + grad_first
    )
    attn_summed = (
        lax.psum_scatter(grad_proj, ("dp", "fsdp"), scatter_dimension=0, tiled=True),
        lax.psum_scatter(grad_out, ("dp", "fsdp"), scatter_dimension=0, tiled=True),
        lax.psum_scatter(grad_gain_one, ("dp", "fsdp"), scatter_dimension=0, tiled=True),
        lax.psum_scatter(grad_bias_one, ("dp", "fsdp"), scatter_dimension=0, tiled=True),
    )
    return (
        x_out,
        y_out,
        grad_input,
        attn_summed[0],
        attn_summed[1],
        attn_summed[2],
        attn_summed[3],
        ffn_summed[0],
        ffn_summed[1],
        ffn_summed[2],
        ffn_summed[3],
        ffn_summed[4],
    )


def solution(mesh):
    return jax.shard_map(
        on_device,
        mesh=mesh,
        in_specs=(
            P(("dp", "fsdp"), None),
            P(("dp", "fsdp"), None),
            P(("dp", "fsdp"), None),
            P(("dp", "fsdp"), None),
            P(("dp", "fsdp"), None),
            P(("dp", "fsdp")),
            P(("dp", "fsdp")),
            P(("dp", "fsdp"), None),
            P(("dp", "fsdp")),
            P(("dp", "fsdp"), None),
            P(("dp", "fsdp")),
            P(("dp", "fsdp")),
            P(("dp", "fsdp"), None),
            P(("dp", "fsdp"), None),
        ),
        out_specs=(
            P(("dp", "fsdp"), None),
            P(("dp", "fsdp"), None),
            P(("dp", "fsdp"), None),
            P(("dp", "fsdp"), None),
            P(("dp", "fsdp"), None),
            P(("dp", "fsdp")),
            P(("dp", "fsdp")),
            P(("dp", "fsdp"), None),
            P(("dp", "fsdp")),
            P(("dp", "fsdp"), None),
            P(("dp", "fsdp")),
            P(("dp", "fsdp")),
        ),
        check_vma=False,
    )
```

profile of v0, /device:TPU:0, one launch (start us, length us, event | category | flops | bytes accessed | tf_op | source)
XLA Modules:
  0.0 793.6 jit_solution(16226759306370055602)
XLA Ops:
  15.1 42.2 %all-reduce.11 = (bf16[512]{0:T(512)(128)(2,1)S(1)}, bf16[512]{0:T(512)(128)(2,1)S(1)}, bf16[2048]{0:T(1024)(128)(2,1)S(1)}, bf16[512]{0:T(512)(128)(2,1)S(1)}, bf16[512]{0:T(512)(128)(2,1)S(1)}) all-reduce(bf16[512]{0:T(512)(128)(2,1)S(1)} %dynamic-update-slice.1, ...), channel_id=1, replica_groups=mesh['dp'=4,'fsdp'=8] {'dp','fsdp'}, use_global_device_ids=true, to_apply=%add.1 | all-reduce | flops 4096 | bytes 16384
  61.1 44.8 %all_gather.32 = bf16[512,512]{1,0:T(8,128)(2,1)} all-gather(bf16[16,512]{1,0:T(8,128)(2,1)} %param.18), channel_id=1, replica_groups=mesh['dp'=4,'fsdp'=8] {'dp','fsdp'}, dimensions={0}, use_global_device_ids=true | all-gather | bytes 540672 | tf_op jit(solution)/shard_map/all_gather | solution.py:69
  128.8 11.1 %fusion.75 = (f32[8,512]{1,0:T(8,128)}, f32[8,512,1024]{2,1,0:T(8,128)}) fusion(pred[512,1024]{1,0:T(8,128)(4,1)} %get-tuple-element.96, bf16[512,8,64]{0,2,1:T(8,128)(2,1)} %bitcast.77, bf16[1024,8,64]{0,2,1:T(8,128)(2,1)S(1)} %bitcast.71), kind=kOutput, calls=%fused_computation.116 | convolution fusion | flops 553649152 | bytes 18890752 | tf_op jit(solution)/shard_map/sub | solution.py:86
  139.9 10.1 %fusion.76 = (f32[8,512]{1,0:T(8,128)}, f32[8,512,1024]{2,1,0:T(8,128)}) fusion(pred[512,1024]{1,0:T(8,128)(4,1)S(1)} %copy-done.24, bf16[512,8,64]{0,2,1:T(8,128)(2,1)S(1)} %bitcast.79, bf16[1024,8,64]{0,2,1:T(8,128)(2,1)S(1)} %bitcast.72), kind=kOutput, calls=%fused_computation.117 | convolution fusion | flops 553649152 | bytes 18890752 | tf_op jit(solution)/shard_map/sub | solution.py:86
  150.0 9.7 %fusion.41 = bf16[512,8,64]{0,2,1:T(8,128)(2,1)} fusion(bf16[1024,8,64]{0,2,1:T(8,128)(2,1)} %bitcast.83, f32[8,512,1024]{2,1,0:T(8,128)} %get-tuple-element.100, f32[8,512]{1,0:T(8,128)} %get-tuple-element.99), kind=kOutput, calls=%fused_computation.77 | convolution fusion | flops 545521664 | bytes 18366464 | tf_op jit(solution)/shard_map/hqk,khd->qhd/dot_general | solution.py:90
  161.1 5.1 fusion.44
  170.7 9.5 %multiply_convert_fusion.2 = (bf16[1024,2048]{1,0:T(8,128)(2,1)}, f32[1024,2048]{1,0:T(8,128)}) fusion(f32[2048]{0:T(1024)S(1)} %copy-done.37, bf16[512,2048]{1,0:T(8,128)(2,1)} %all-gather.6.cloned.1.call-done, f32[1024,512]{0,1:T(8,128)S(1)} %get-tuple-element.83, f32[512]{0:T(512)S(1)} %copy-done.39, f32[512]{0:T(512)S(1)} %copy-done.32, ...), kind=kOutput, calls=%fused_computation.22 | convolution fusion | flops 2171076608 | bytes 16797696 | tf_op jit(solution)/shard_map/dot_general | solution.py:110
  180.2 5.1 all-gather.8.cloned.1.call-done
  185.3 8.3 %fusion.68 = (f32[1024]{0:T(1024)S(1)}, f32[1024,512]{0,1:T(8,128)S(1)}, f32[1024,512]{0,1:T(8,128)}) fusion(f32[512]{0:T(512)S(1)} %copy-done.39, f32[512]{0:T(512)S(1)} %copy-done.32, f32[1024]{0:T(1024)S(1)} %fusion.50, f32[1024,512]{0,1:T(8,128)S(1)} %get-tuple-element.83, f32[1024]{0:T(1024)S(1)} %broadcast_multiply_fusion.1, f32[1024]{0:T(1024)S(1)} %fusion.49, ...), kind=kOutput, calls=%fused_computation.110 | convolution fusion | flops 2152201216 | bytes 16797696 | tf_op jit(solution)/shard_map/dot_general | solution.py:114
  198.8 8.7 %convert_reduce_fusion = (f32[2048]{0:T(1024)}, bf16[1024,2048]{1,0:T(8,128)(2,1)S(1)}) fusion(f32[1024,2048]{1,0:T(8,128)S(1)} %copy-done.47, f32[2048]{0:T(1024)S(1)} %copy-done.37, bf16[1024,512]{0,1:T(8,128)(2,1)S(1)} %get-tuple-element.88, bf16[2048,512]{1,0:T(8,128)(2,1)S(1)} %copy-done.44), kind=kOutput, calls=%fused_computation.21 | convolution fusion | flops 2195716096 | bytes 15745024 | tf_op jit(solution)/shard_map/td,fd->tf/dot_general | solution.py:135
  218.3 10.7 %multiply_reduce_fusion.1 = (f32[8,512]{1,0:T(8,128)S(1)}, f32[8,512,1024]{2,1,0:T(8,128)}) fusion(f32[8,512,1024]{2,1,0:T(8,128)} %get-tuple-element.102, f32[8,512]{1,0:T(8,128)S(1)} %copy-done.27, bf16[512,8,64]{0,2,1:T(8,128)(2,1)S(1)} %bitcast.89, bf16[1024,8,64]{0,2,1:T(8,128)(2,1)S(1)} %bitcast.85), kind=kOutput, calls=%fused_computation.5 | convolution fusion | flops 549449728 | bytes 35160064 | tf_op jit(solution)/shard_map/qhd,khd->hqk/dot_general | solution.py:180
  229.0 11.6 %multiply_convert_fusion.1 = bf16[8,512,1024]{2,1,0:T(8,128)(2,1)S(1)} fusion(f32[8,512,1024]{2,1,0:T(8,128)} %get-tuple-element.108, f32[8,512]{1,0:T(8,128)S(1)} %get-tuple-element.107, f32[8,512,1024]{2,1,0:T(8,128)} %get-tuple-element.102, f32[8,512]{1,0:T(8,128)S(1)} %copy-done.27), kind=kLoop, calls=%fused_computation.4 | loop fusion | flops 16777216 | bytes 41975808 | tf_op jit(solution)/shard_map/convert_element_type | solution.py:184
  247.0 8.2 %fusion.17 = f32[8,64,1024]{2,1,0:T(8,128)} fusion(bf16[512,8,64]{0,2,1:T(8,128)(2,1)S(1)} %bitcast.91, f32[8,512,1024]{2,1,0:T(8,128)} %get-tuple-element.100, f32[8,512]{1,0:T(8,128)S(1)} %copy-done.28), kind=kOutput, calls=%fused_computation.31 | convolution fusion | flops 545259520 | bytes 19415040 | tf_op jit(solution)/shard_map/hqk,qhd->khd/dot_general | solution.py:177
  255.2 10.7 %multiply_reduce_fusion = (f32[8,512]{1,0:T(8,128)S(1)}, f32[8,512,1024]{2,1,0:T(8,128)}) fusion(f32[8,512,1024]{2,1,0:T(8,128)} %get-tuple-element.100, f32[8,512]{1,0:T(8,128)S(1)} %copy-done.28, bf16[512,8,64]{0,2,1:T(8,128)(2,1)S(1)} %bitcast.92, bf16[1024,8,64]{0,2,1:T(8,128)(2,1)S(1)} %bitcast.86), kind=kOutput, calls=%fused_computation.3 | convolution fusion | flops 549449728 | bytes 35160064 | tf_op jit(solution)/shard_map/qhd,khd->hqk/dot_general | solution.py:180
  266.0 11.6 %multiply_convert_fusion = bf16[8,512,1024]{2,1,0:T(8,128)(2,1)S(1)} fusion(f32[8,512,1024]{2,1,0:T(8,128)} %get-tuple-element.110, f32[8,512]{1,0:T(8,128)S(1)} %get-tuple-element.109, f32[8,512,1024]{2,1,0:T(8,128)} %get-tuple-element.100, f32[8,512]{1,0:T(8,128)S(1)} %copy-done.28), kind=kLoop, calls=%fused_computation.2 | loop fusion | flops 16777216 | bytes 41975808 | tf_op jit(solution)/shard_map/convert_element_type | solution.py:184
  282.9 7.5 add_convert_fusion
  299.2 6.6 fusion.62
  307.0 6.6 fusion.79
  316.1 38.9 %all-reduce.10 = (f32[512]{0:T(512)S(1)}, f32[512]{0:T(512)S(1)}, f32[2048]{0:T(1024)S(1)}, f32[512]{0:T(512)S(1)}, f32[512]{0:T(512)S(1)}) all-reduce(f32[512]{0:T(512)S(1)} %copy-done.41, f32[512]{0:T(512)S(1)} %copy-done.42, f32[2048]{0:T(1024)S(1)} %copy-done.38, ...), channel_id=4, replica_groups=mesh['dp'=4,'fsdp'=8] {'dp','fsdp'}, use_global_device_ids=true, to_apply=%region_19.20.clone | all-reduce | flops 4096 | bytes 32768
  360.4 5.2 add_add_fusion.2
  369.1 30.6 %reduce-scatter.7.cloned.1.call-done = f32[16,512]{1,0:T(8,128)} async-done(((f32[512,512]{1,0:T(8,128)}), f32[16,512]{1,0:T(8,128)}) %reduce-scatter.7.cloned.1.call-update) | async-done | bytes 32784 | tf_op jit(solution)/shard_map/reduce_scatter | solution.py:210
  399.7 104.4 %reduce-scatter.13.cloned.1.call-done = f32[16,1536]{1,0:T(8,128)} async-done(((f32[512,1536]{1,0:T(8,128)}), f32[16,1536]{1,0:T(8,128)}) %reduce-scatter.13.cloned.1.call-update) | async-done | bytes 98320
  504.1 142.5 %reduce-scatter.9.cloned.1.call-done = f32[16,2048]{1,0:T(8,128)} async-done(((f32[512,2048]{1,0:T(8,128)}), f32[16,2048]{1,0:T(8,128)}) %reduce-scatter.9.cloned.1.call-update) | async-done | bytes 131088 | tf_op jit(solution)/shard_map/reduce_scatter | solution.py:146
  646.7 139.7 %reduce-scatter.11.cloned.1.call-done = f32[64,512]{1,0:T(8,128)} async-done(((f32[2048,512]{1,0:T(8,128)}), f32[64,512]{1,0:T(8,128)}) %reduce-scatter.11.cloned.1.call-update) | async-done | bytes 131088 | tf_op jit(solution)/shard_map/reduce_scatter | solution.py:148
  (188 shorter events, 89.4 us)
Async XLA Ops:
  7.2 108.7 %all-gather.4.cloned.1.call-start = ((), (), s32[]{:S(2)}) async-start(), calls=%async_computation.4 | async-start | bytes 1622016 | tf_op jit(solution)/shard_map/all_gather | solution.py:68
  7.9 162.4 %all-gather.6.cloned.1.call-start = ((), (), s32[]{:S(2)}) async-start(), calls=%async_computation.5 | async-start | bytes 2162688 | tf_op jit(solution)/shard_map/all_gather | solution.py:102
  8.7 176.6 %all-gather.8.cloned.1.call-start = ((), (), s32[]{:S(2)}) async-start(), calls=%async_computation.6 | async-start | bytes 2162688 | tf_op jit(solution)/shard_map/all_gather | solution.py:104
  9.4 390.3 %reduce-scatter.7.cloned.1.call-start = ((), (), s32[]{:S(2)}) async-start(), calls=%async_computation.7 | async-start | bytes 1081344 | tf_op jit(solution)/shard_map/reduce_scatter | solution.py:210
  59.0 50.8 %copy-start.31 = (s32[1024]{0:T(1024)}, s32[1024]{0:T(1024)S(1)}, u32[]{:S(2)}) copy-start(s32[1024]{0:T(1024)S(1)} %iota.30) | copy-start | bytes 12292
  107.4 4.7 copy-start.16
  123.0 16.9 %copy-start.2 = (bf16[1024,512]{0,1:T(8,128)(2,1)}, bf16[1024,512]{0,1:T(8,128)(2,1)S(1)}, u32[]{:S(2)}) copy-start(bf16[1024,512]{0,1:T(8,128)(2,1)S(1)} %copy.83) | copy-start | bytes 3145732
  128.8 11.1 %copy-start.12 = (bf16[512,512]{0,1:T(8,128)(2,1)S(1)}, bf16[512,512]{0,1:T(8,128)(2,1)}, u32[]{:S(2)}) copy-start(bf16[512,512]{0,1:T(8,128)(2,1)} %copy.82) | copy-start | bytes 1572868
  128.8 11.1 %copy-start.24 = (pred[512,1024]{1,0:T(8,128)(4,1)S(1)}, pred[512,1024]{1,0:T(8,128)(4,1)}, u32[]{:S(2)}) copy-start(pred[512,1024]{1,0:T(8,128)(4,1)} %get-tuple-element.95) | copy-start | bytes 1572868
  150.0 11.1 %copy-start = (f32[8,512,1024]{2,1,0:T(8,128)S(1)}, f32[8,512,1024]{2,1,0:T(8,128)}, u32[]{:S(2)}) copy-start(f32[8,512,1024]{2,1,0:T(8,128)} %get-tuple-element.102) | copy-start | bytes 50331652
  170.3 41.2 %copy-start.29 = (f32[1024]{0:T(1024)}, f32[1024]{0:T(1024)S(1)}, u32[]{:S(2)}) copy-start(f32[1024]{0:T(1024)S(1)} %fusion.50) | copy-start | bytes 12292
  185.3 13.5 %copy-start.47 = (f32[1024,2048]{1,0:T(8,128)S(1)}, f32[1024,2048]{1,0:T(8,128)}, u32[]{:S(2)}) copy-start(f32[1024,2048]{1,0:T(8,128)} %get-tuple-element.105) | copy-start | bytes 25165828
  198.8 8.7 %copy-start.21 = (bf16[1024,512]{0,1:T(8,128)(2,1)}, bf16[1024,512]{0,1:T(8,128)(2,1)S(1)}, u32[]{:S(2)}) copy-start(bf16[1024,512]{0,1:T(8,128)(2,1)S(1)} %get-tuple-element.88) | copy-start | bytes 3145732
  198.8 8.7 %copy-start.43 = (bf16[512,2048]{1,0:T(8,128)(2,1)S(1)}, bf16[512,2048]{1,0:T(8,128)(2,1)}, u32[]{:S(2)}) copy-start(bf16[512,2048]{1,0:T(8,128)(2,1)} %all-gather.6.cloned.1.call-done) | copy-start | bytes 6291460
  207.5 4.0 copy-start.46
  218.3 10.7 %copy-start.25 = (bf16[512,512]{0,1:T(8,128)(2,1)}, bf16[512,512]{0,1:T(8,128)(2,1)S(1)}, u32[]{:S(2)}) copy-start(bf16[512,512]{0,1:T(8,128)(2,1)S(1)} %get-tuple-element.91) | copy-start | bytes 1572868
  229.0 11.6 %copy-start.3 = (bf16[1024,512]{0,1:T(8,128)(2,1)S(1)}, bf16[1024,512]{0,1:T(8,128)(2,1)}, u32[]{:S(2)}) copy-start(bf16[1024,512]{0,1:T(8,128)(2,1)} %copy-done.2) | copy-start | bytes 3145732
  240.6 3.5 copy-start.13
  265.9 238.2 %reduce-scatter.13.cloned.1.call-start = ((), (), s32[]{:S(2)}) async-start(), calls=%async_computation.10 | async-start | bytes 3244032
  282.9 7.5 copy-start.20
  282.9 8.5 %copy-start.18 = (bf16[1024,512]{1,0:T(8,128)(2,1)S(1)}, bf16[1024,512]{1,0:T(8,128)(2,1)}, u32[]{:S(2)}) copy-start(bf16[1024,512]{1,0:T(8,128)(2,1)} %param.14) | copy-start | bytes 3145732
  298.5 348.1 %reduce-scatter.9.cloned.1.call-start = ((), (), s32[]{:S(2)}) async-start(), calls=%async_computation.8 | async-start | bytes 4325376 | tf_op jit(solution)/shard_map/reduce_scatter | solution.py:146
  305.8 480.5 %reduce-scatter.11.cloned.1.call-start = ((), (), s32[]{:S(2)}) async-start(), calls=%async_computation.9 | async-start | bytes 4325376 | tf_op jit(solution)/shard_map/reduce_scatter | solution.py:148
  357.4 3.0 copy-start.6
  (33 other events, 56.4 us)
Sparse Core Ops, SparseCore 0:
  10.9 57.6 all-gather.3
  71.4 55.6 all-gather.5
  130.0 55.2 all-gather.7
  266.1 133.6 reduce-scatter.6
  406.5 97.6 reduce-scatter.12
  507.0 139.6 reduce-scatter.8
  649.6 136.6 reduce-scatter.10
where the time goes:
time: 803 us; the launch traced here: 794 us
  waiting for transfers between devices  424 us (53%)
  matrix products  145 us (18%)
  blocking collectives  126 us (16%)
  local copies, waits for them, and re-layouts  45.3 us (6%)
  other arithmetic  37.1 us (5%)
  between operations  15.1 us (2%)
    reduce_scatter x1, waiting for transfers between devices, on_device(): lax.psum_scatter(grad_up, ('dp', 'fsdp'), scatter_dimension=0, tiled=True)  143 us
    reduce_scatter x1, waiting for transfers between devices, on_device(): lax.psum_scatter(grad_down, ('dp', 'fsdp'), scatter_dimension=0, tiled=True)  140 us
    unnamed x8, waiting for transfers between devices  107 us
    unnamed x2, blocking collectives  81.1 us
    all_gather x1, blocking collectives, on_device(): lax.all_gather(w_out, ('dp', 'fsdp'), axis=0, tiled=True)  44.8 us
    unnamed x121, local copies, waits for them, and re-layouts  34.5 us
    reduce_scatter x1, waiting for transfers between devices, on_device(): lax.psum_scatter(grad_out, ('dp', 'fsdp'), scatter_dimension=0, tiled=True)  30.6 us
    convert_element_type x2, other arithmetic, on_device(): grad_scores = grad_scores.astype(jnp.bfloat16)  23.2 us
  transfers between devices with their start and end apart: 7, of which 5 were waited for; matrix products, arithmetic and copies ran while one was open for 18% of the time, Pallas kernels for 0%

commit v1 on v0

v1 whole, which is shorter than its diff:
```python
import functools

import jax
import jax.numpy as jnp
from jax import lax
from jax.experimental import pallas as pl
from jax.experimental.pallas import tpu as pltpu
from jax.sharding import PartitionSpec as P

H = 8
PAIR = 128
HALF = 64
BLOCK = 256
CHUNK = 512
GRID = (4, 2, 2, 2)
ROWS = 16
Z = GRID[0]
PIECES = 12
VMEM_LIMIT = 67000000
EPSILON = 1e-05
NEGATIVE = -1e30
GELU_C = 0.7978845608028654
GELU_K = 0.044715
F32 = jnp.float32
BF16 = jnp.bfloat16
MESH = pl.DeviceIdType.MESH


def mm(a, b):
    return lax.dot_general(a, b, (((1,), (0,)), ((), ())), preferred_element_type=F32)


def mm_nt(a, b):
    return lax.dot_general(a, b, (((1,), (1,)), ((), ())), preferred_element_type=F32)


def mm_tn(a, b):
    return lax.dot_general(a, b, (((0,), (0,)), ((), ())), preferred_element_type=F32)


class Place:
    def __init__(self):
        self.z = lax.axis_index("dp")
        inner = lax.axis_index("fsdp")
        self.c = lax.rem(inner, 2)
        self.x = lax.rem(inner // 2, 2)
        self.y = inner // 4

    def device(self, z, y, x, c):
        return (z, (y * 2 + x) * 2 + c)

    def first(self, p):
        odd = p % 2
        return (self.y + odd) % 2, (self.x + 1 - odd) % 2

    def second(self, p):
        odd = p % 2
        return (self.y + 1 - odd) % 2, (self.x + odd) % 2

    def around(self, d):
        return lax.rem(self.z + d, Z)


class Gather:
    def __init__(self, place, buf, send, recv):
        self.at, self.buf, self.send, self.recv = place, buf, send, recv

    def copy(self, block, target, p, n):
        ref = self.buf.at[block]
        return pltpu.make_async_remote_copy(
            src_ref=ref,
            dst_ref=ref,
            send_sem=self.send.at[p, n],
            recv_sem=self.recv.at[p, n],
            device_id=target,
            device_id_type=MESH,
        )

    def along_z(self, p, d, source):
        a = self.at
        return self.copy((p, source, a.y, a.x, a.c), a.device(a.around(d), a.y, a.x, a.c), p, d - 1)

    def plane(self, p, n, y, x, to):
        a = self.at
        return self.copy((p, slice(None), y, x, a.c), a.device(a.z, to[0], to[1], a.c), p, n)

    def core(self, p, c):
        a = self.at
        every = slice(None)
        return self.copy((p, every, every, every, c), a.device(a.z, a.y, a.x, 1 - a.c), p, Z + 2)

    def step(self, n, p):
        a = self.at
        y1, x1 = a.first(p)
        y2, x2 = a.second(p)
        if n == 0:
            for d in range(1, Z):
                self.along_z(p, d, a.z).start()
        elif n == 1:
            for d in range(1, Z):
                self.along_z(p, d, a.around(Z - d)).wait_recv()
            self.plane(p, Z - 1, a.y, a.x, (y1, x1)).start()
            self.plane(p, Z, a.y, a.x, (y2, x2)).start()
        elif n == 2:
            self.plane(p, Z - 1, y1, x1, (y1, x1)).wait_recv()
            self.plane(p, Z + 1, y1, x1, (y2, x2)).start()
        elif n == 3:
            self.plane(p, Z, y2, x2, (y2, x2)).wait_recv()
            self.plane(p, Z + 1, 1 - a.y, 1 - a.x, (y2, x2)).wait_recv()
            self.core(p, a.c).start()
        elif n == 4:
            self.core(p, 1 - a.c).wait_recv()
        else:
            for d in range(1, Z):
                self.along_z(p, d, a.z).wait_send()
            self.plane(p, Z - 1, a.y, a.x, (y1, x1)).wait_send()
            self.plane(p, Z, a.y, a.x, (y2, x2)).wait_send()
            self.plane(p, Z + 1, y1, x1, (y2, x2)).wait_send()
            self.core(p, a.c).wait_send()


class Scatter:
    def __init__(self, place, buf, got_core, got_first, got_second, got_z, send, recv, finish):
        self.at, self.buf = place, buf
        self.got_core, self.got_first = got_core, got_first
        self.got_second, self.got_z = got_second, got_z
        self.send, self.recv, self.finish = send, recv, finish

    def copy(self, src, dst, target, p, n):
        return pltpu.make_async_remote_copy(
            src_ref=src,
            dst_ref=dst,
            send_sem=self.send.at[p, n],
            recv_sem=self.recv.at[p, n],
            device_id=target,
            device_id_type=MESH,
        )

    def core(self, p):
        a = self.at
        every = slice(None)
        return self.copy(
            self.buf.at[p, every, every, every, 1 - a.c],
            self.got_core.at[p],
            a.device(a.z, a.y, a.x, 1 - a.c),
            p,
            0,
        )

    def plane(self, p, n, y, x, to):
        a = self.at
        dst = self.got_second.at[p] if n == 3 else self.got_first.at[p, n - 1]
        target = a.device(a.z, to[0], to[1], a.c)
        return self.copy(self.buf.at[p, :, y, x, a.c], dst, target, p, n)

    def along_z(self, p, d):
        a = self.at
        z = a.around(d)
        return self.copy(
            self.buf.at[p, z, a.y, a.x, a.c],
            self.got_z.at[p, d - 1],
            a.device(z, a.y, a.x, a.c),
            p,
            3 + d,
        )

    def add(self, block, value):
        self.buf[block] = (self.buf[block].astype(F32) + value.astype(F32)).astype(BF16)

    def step(self, n, p):
        a = self.at
        y1, x1 = a.first(p)
        y2, x2 = a.second(p)
        every = slice(None)
        if n == 0:
            self.core(p).start()
        elif n == 1:
            self.core(p).wait_recv()
            self.add((p, every, every, every, a.c), self.got_core[p])
            self.plane(p, 1, 1 - a.y, 1 - a.x, (y1, x1)).start()
            self.plane(p, 2, y1, x1, (y1, x1)).start()
        elif n == 2:
            self.plane(p, 1, 1 - a.y, 1 - a.x, (y1, x1)).wait_recv()
            self.add((p, every, y2, x2, a.c), self.got_first[p, 0])
            self.plane(p, 3, y2, x2, (y2, x2)).start()
            self.plane(p, 2, y1, x1, (y1, x1)).wait_recv()
            self.add((p, every, a.y, a.x, a.c), self.got_first[p, 1])
        elif n == 3:
            self.plane(p, 3, y2, x2, (y2, x2)).wait_recv()
            self.add((p, every, a.y, a.x, a.c), self.got_second[p])
            for d in range(1, Z):
                self.along_z(p, d).start()
        elif n == 4:
            total = self.buf[p, a.z, a.y, a.x, a.c].astype(F32)
            for d in range(1, Z):
                self.along_z(p, d).wait_recv()
                total = total + self.got_z[p, d - 1].astype(F32)
            self.finish(p, total)
        else:
            self.core(p).wait_send()
            self.plane(p, 1, 1 - a.y, 1 - a.x, (y1, x1)).wait_send()
            self.plane(p, 2, y1, x1, (y1, x1)).wait_send()
            self.plane(p, 3, y2, x2, (y2, x2)).wait_send()
            for d in range(1, Z):
                self.along_z(p, d).wait_send()


def as_matrix(value):
    return value.reshape(-1, value.shape[-1])


def layer_kernel(linked, *refs):
    refs = list(refs)

    def take(n):
        out = refs[:n]
        del refs[:n]
        return out

    lengths_ref, x_hbm, y_hbm, gx_hbm, gy_hbm = take(5)
    if linked:
        s_qkv, s_out, s_up, s_down, s_small = take(5)
        xo_hbm, yo_hbm, dx_hbm, o_qkv, o_out, o_up, o_down, o_small = take(8)
        weights, grads, small, g_small = take(4)
        got = take(8)
        sems = take(8)
    else:
        weights, small = take(2)
        xo_hbm, yo_hbm, dx_hbm, grads, g_small = take(5)
    (
        x_ref,
        y_buf,
        gx_buf,
        gy_buf,
        dx_ref,
        params,
        sums,
        qkv_ref,
        att_t,
        datt,
        datt_t,
        probs,
        bias,
        hidden,
        du_ref,
        x_low,
        df_ref,
        x_t,
        s_scr,
        in_sem,
        out_sem,
    ) = refs

    slots, width = x_ref.shape
    nblk = slots // BLOCK
    ff = hidden.shape[1]
    pairs = H // 2
    per = ff // CHUNK

    loads = []
    for n, (src, dst) in enumerate(
        ((x_hbm, x_ref), (y_hbm, y_buf), (gx_hbm, gx_buf), (gy_hbm, gy_buf))
    ):
        cp = pltpu.make_async_copy(src, dst, in_sem.at[n])
        cp.start()
        loads.append(cp)

    if linked:
        place = Place()
        z, y, x, c = place.z, place.y, place.x, place.c
        barrier = pltpu.get_barrier_semaphore()
        partners = [
            place.device(z, y, x, 1 - c),
            place.device(z, y, 1 - x, c),
            place.device(z, 1 - y, x, c),
        ] + [place.device(place.around(d), y, x, c) for d in range(1, Z)]
        for partner in partners:
            pl.semaphore_signal(barrier, inc=1, device_id=partner, device_id_type=MESH)
        for g in range(pairs):
            lanes = [slice(n * width + g * PAIR, n * width + (g + 1) * PAIR) for n in range(3)]
            own = [s_qkv[:, lane] for lane in lanes] + [s_out[:, lanes[0]]]
            weights[g, z, y, x, c] = jnp.concatenate(own, axis=1)
        for j in range(per):
            weights[pairs + j, z, y, x, c] = s_up[:, j * CHUNK : (j + 1) * CHUNK]
            weights[pairs + per + j, z, y, x, c] = s_down[j * ROWS : (j + 1) * ROWS, :]
        small[0, z, y, x, c] = s_small[...]
        pl.semaphore_wait(barrier, len(partners))

        def finish(p, total):
            if isinstance(p, int):
                if p < pairs:
                    for n in range(3):
                        lane = slice(n * width + p * PAIR, n * width + (p + 1) * PAIR)
                        o_qkv[:, lane] = total[:, n * PAIR : (n + 1) * PAIR]
                    o_out[:, p * PAIR : (p + 1) * PAIR] = total[:, 3 * PAIR :]
                elif p < pairs + per:
                    o_up[:, (p - pairs) * CHUNK : (p - pairs + 1) * CHUNK] = total
                else:
                    at = (p - pairs - per) * ROWS
                    o_down[at : at + ROWS, :] = total

        def finish_small(p, total):
            o_small[...] = total

        gather = Gather(place, weights, sems[0], sems[1])
        gather_small = Gather(place, small, sems[2], sems[3])
        scatter = Scatter(place, grads, *got[:4], sems[4], sems[5], finish)
        scatter_small = Scatter(place, g_small, *got[4:], sems[6], sems[7], finish_small)
        for n in range(5):
            gather_small.step(n, 0)
            for p in range(PIECES):
                gather.step(n, p)

    def segments(pos):
        seg = jnp.zeros(pos.shape, jnp.int32)
        end = jnp.int32(0)
        for j in range(lengths_ref.shape[1]):
            end = end + lengths_ref[0, j]
            seg = seg + (end <= pos).astype(jnp.int32)
        return jnp.where(pos < end, seg, -1 - pos), end

    starts = [BLOCK * (qb * (qb + 1) // 2) for qb in range(nblk)]
    for qb in range(nblk):
        q_pos = lax.broadcasted_iota(jnp.int32, (1, BLOCK), 1) + qb * BLOCK
        q_seg, total = segments(q_pos)
        for kb in range(qb + 1):
            k_pos = lax.broadcasted_iota(jnp.int32, (BLOCK, 1), 0) + kb * BLOCK
            k_seg, _ = segments(k_pos)
            allowed = k_seg == q_seg
            if kb == qb:
                allowed = allowed & (k_pos <= q_pos)
            at = starts[qb] + kb * BLOCK
            bias[at : at + BLOCK, :] = jnp.where(allowed, 0.0, NEGATIVE).astype(F32)

    loads[0].wait()
    x_t[...] = x_ref[...].T

    def spread(first, at, r):
        rows = first.shape[0]
        column = lax.broadcasted_iota(jnp.int32, (PAIR, width), 1)
        pick = (lax.broadcasted_iota(jnp.int32, (PAIR, width), 0) == at + column % r).astype(BF16)
        own = lax.broadcasted_iota(jnp.int32, (rows, width), 0)
        mine = own == (lax.broadcasted_iota(jnp.int32, (rows, width), 1) // r) * ROWS
        return jnp.sum(jnp.where(mine, mm(first, pick), 0.0), axis=0, keepdims=True)

    blocks = as_matrix(small[0])
    for n in range(4):
        params[n : n + 1, :width] = spread(blocks, n * ROWS, ROWS)
    for j in range(per):
        rows = blocks.shape[0] // per
        params[4:5, j * CHUNK : (j + 1) * CHUNK] = spread(
            blocks[j * rows : (j + 1) * rows], 4 * ROWS, ff * ROWS // width
        )

    lane = lax.broadcasted_iota(jnp.int32, (BLOCK, PAIR), 1)
    sub = lax.broadcasted_iota(jnp.int32, (PAIR, BLOCK), 0)

    def one_head(index, value, a):
        keep = index < HALF if a == 0 else index >= HALF
        return jnp.where(keep, value.astype(F32), 0.0).astype(BF16)

    def w_qkv(g):
        return as_matrix(weights[g, ..., : 3 * PAIR])

    def w_out():
        return jnp.concatenate(
            [as_matrix(weights[g, ..., 3 * PAIR :]) for g in range(pairs)], axis=1
        )

    def w_up(j):
        return as_matrix(weights[pairs + j])

    def w_down(j):
        parts = [weights[pairs + per + n, j].reshape(-1, ROWS, width) for n in range(per)]
        return as_matrix(jnp.stack(parts, axis=1))

    def attend(g, carry):
        for qb in range(nblk):
            rows = slice(qb * BLOCK, (qb + 1) * BLOCK)
            part = mm(x_ref[rows, :], w_qkv(g))
            q = part[:, :PAIR].astype(BF16).astype(F32) * (HALF**-0.5)
            qkv_ref[g, rows, :] = jnp.concatenate([q, part[:, PAIR:]], axis=1).astype(BF16)
        v_t = qkv_ref[g, :, 2 * PAIR :].T
        for qb in range(nblk):
            for a in range(2):
                rows = slice(qb * BLOCK, (qb + 1) * BLOCK)
                q = one_head(lane, qkv_ref[g, rows, :PAIR], a)
                top = None
                for kb in range(qb + 1):
                    k = qkv_ref[g, kb * BLOCK : (kb + 1) * BLOCK, PAIR : 2 * PAIR]
                    at = starts[qb] + kb * BLOCK
                    s = mm_nt(k, q) + bias[at : at + BLOCK, :]
                    s_scr[a, kb] = s
                    high = jnp.max(s, axis=0, keepdims=True)
                    top = high if top is None else jnp.maximum(top, high)
                whole = None
                for kb in range(qb + 1):
                    e = jnp.exp(s_scr[a, kb] - top)
                    s_scr[a, kb] = e
                    one = jnp.sum(e, axis=0, keepdims=True)
                    whole = one if whole is None else whole + one
                inverse = 1.0 / whole
                out = None
                for kb in range(qb + 1):
                    at = starts[qb] + kb * BLOCK
                    p = (s_scr[a, kb] * inverse).astype(BF16)
                    probs[2 * g + a, at : at + BLOCK, :] = p
                    o = mm(v_t[a * HALF : (a + 1) * HALF, kb * BLOCK : (kb + 1) * BLOCK], p)
                    out = o if out is None else out + o
                att_t[g, a * HALF : (a + 1) * HALF, rows] = out.astype(BF16)
        return carry

    lax.fori_loop(0, pairs, attend, 0)

    for cp in loads[1:]:
        cp.wait()

    sums[...] = jnp.zeros_like(sums)
    gain_one = params[0:1, :width]
    bias_one = params[1:2, :width]
    gain_two = params[2:3, :width]
    bias_two = params[3:4, :width]

    def norm(value):
        mean = jnp.mean(value, axis=1, keepdims=True)
        centred = value - mean
        var = jnp.mean(centred * centred, axis=1, keepdims=True)
        inv = lax.rsqrt(var + EPSILON)
        return centred * inv, inv

    def norm_back(grad, gain, n, inv):
        gn = grad * gain
        m1 = jnp.mean(gn, axis=1, keepdims=True)
        m2 = jnp.mean(gn * n, axis=1, keepdims=True)
        return (gn - m1 - n * m2) * inv

    def add_sum(row, at, value):
        sums[row : row + 1, at : at + value.shape[1]] += jnp.sum(value, axis=0, keepdims=True)

    def out_copies(rows, i):
        return (
            pltpu.make_async_copy(gx_buf.at[rows, :], xo_hbm.at[rows, :], out_sem.at[0, i]),
            pltpu.make_async_copy(y_buf.at[rows, :], yo_hbm.at[rows, :], out_sem.at[1, i]),
        )

    def slab(j, n):
        return divmod(j * (CHUNK // BLOCK) + n, nblk)

    def rows_of_tile(i, carry):
        r0 = pl.multiple_of(i * BLOCK, BLOCK)
        rows = pl.ds(r0, BLOCK)
        at_tile = att_t[:, :, rows].reshape(width, BLOCK).T
        branch_a = mm(at_tile, w_out())
        n1, inv1 = norm(x_ref[rows, :].astype(F32) + branch_a)
        x_mid = n1 * gain_one + bias_one
        xl = x_mid.astype(BF16)
        x_low[rows, :] = xl
        branch_f = None
        for j in range(per):
            cols = slice(j * CHUNK, (j + 1) * CHUNK)
            u = mm(xl, w_up(j)) + params[4:5, cols]
            u2 = u * u
            t = jnp.tanh(u * (GELU_C + (GELU_C * GELU_K) * u2))
            h = 0.5 + 0.5 * t
            low = (u * h).astype(BF16)
            hidden[rows, cols] = low
            slope = h + h * (1.0 - h) * (u * (2.0 * GELU_C + (6.0 * GELU_C * GELU_K) * u2))
            for n in range(CHUNK // BLOCK):
                s_scr[slab(j, n)] = slope[:, n * BLOCK : (n + 1) * BLOCK]
            part = mm(low, w_down(j))
            branch_f = part if branch_f is None else branch_f + part
        n2, inv2 = norm(x_mid + branch_f)
        live = (lax.broadcasted_iota(jnp.int32, (BLOCK, width), 0) + r0) < total
        gx = jnp.where(live, gx_buf[rows, :].astype(F32), 0.0)
        gy = jnp.where(live, gy_buf[rows, :].astype(F32), 0.0)
        gx_buf[rows, :] = jnp.where(live, n2 * gain_two + bias_two, 0.0).astype(BF16)
        y_buf[rows, :] = jnp.where(live, y_buf[rows, :] + branch_a + branch_f, 0.0)
        for cp in out_copies(rows, i):
            cp.start()
        add_sum(3, 0, gx)
        add_sum(2, 0, gx * n2)
        dr2 = norm_back(gx, gain_two, n2, inv2)
        df = (dr2 + gy).astype(BF16)
        df_ref[rows, :] = df
        dx_mid = dr2
        for j in range(per):
            cols = slice(j * CHUNK, (j + 1) * CHUNK)
            slope = jnp.concatenate([s_scr[slab(j, n)] for n in range(CHUNK // BLOCK)], axis=1)
            du = (mm_nt(df, w_down(j)) * slope).astype(BF16)
            du_ref[rows, cols] = du
            add_sum(4, j * CHUNK, du.astype(F32))
            dx_mid = dx_mid + mm_nt(du, w_up(j))
        add_sum(1, 0, dx_mid)
        add_sum(0, 0, dx_mid * n1)
        dr1 = norm_back(dx_mid, gain_one, n1, inv1)
        dx_ref[rows, :] = dr1
        da = (dr1 + gy).astype(BF16)
        gy_buf[rows, :] = da
        datt[rows, :] = mm_nt(da, w_out()).astype(BF16)
        datt_t[:, :, rows] = mm_nt(w_out(), da).astype(BF16).reshape(pairs, PAIR, BLOCK)
        return carry

    lax.fori_loop(0, nblk, rows_of_tile, 0)

    def put(p, at, value):
        grads[p, ..., at : at + value.shape[1]] = value.astype(BF16).reshape(
            GRID + (ROWS, value.shape[1])
        )

    for j in range(per):
        part = mm_tn(hidden[:, j * CHUNK : (j + 1) * CHUNK], df_ref[...]).astype(BF16)
        part = part.reshape(-1, per, ROWS, width)
        for n in range(per):
            grads[pairs + per + n, j] = part[:, n].reshape(GRID[1:] + (ROWS, width))
    for j in range(per):
        put(pairs + j, 0, mm_tn(x_low[...], du_ref[:, j * CHUNK : (j + 1) * CHUNK]))
    part = mm(att_t[...].reshape(width, slots), gy_buf[...])
    for g in range(pairs):
        put(g, 3 * PAIR, part[:, g * PAIR : (g + 1) * PAIR])

    def gathered(row, at, r):
        value = jnp.broadcast_to(row, (row.shape[1] * ROWS // r, width))
        own = lax.broadcasted_iota(jnp.int32, value.shape, 0) // ROWS
        mine = own == lax.broadcasted_iota(jnp.int32, value.shape, 1) // r
        column = lax.broadcasted_iota(jnp.int32, (width, PAIR), 0)
        pick = (lax.broadcasted_iota(jnp.int32, (width, PAIR), 1) == at + column % r).astype(BF16)
        return mm(jnp.where(mine, value, 0.0).astype(BF16), pick)

    rest = [
        gathered(sums[4:5, j * CHUNK : (j + 1) * CHUNK], 4 * ROWS, ff * ROWS // width)
        for j in range(per)
    ]
    rest = jnp.concatenate(rest, axis=0)
    for n in range(4):
        rest = rest + gathered(sums[n : n + 1, :width], n * ROWS, ROWS)
    g_small[0] = rest.astype(BF16).reshape(GRID + (ROWS, PAIR))

    def attend_back(g, carry):
        k_t = qkv_ref[g, :, PAIR : 2 * PAIR].T
        s_scr[0] = jnp.zeros((nblk, BLOCK, BLOCK), F32)
        lanes = pl.ds(pl.multiple_of(g * PAIR, PAIR), PAIR)
        dq_blocks = []
        for qb in range(nblk):
            rows = slice(qb * BLOCK, (qb + 1) * BLOCK)
            dq_parts = []
            for a in range(2):
                heads = slice(a * HALF, (a + 1) * HALF)
                q = one_head(lane, qkv_ref[g, rows, :PAIR], a)
                do = one_head(lane, datt[rows, lanes], a)
                do_t = one_head(sub, datt_t[g, :, rows], a)
                dots = jnp.sum(
                    att_t[g, heads, rows].astype(F32) * datt_t[g, heads, rows].astype(F32),
                    axis=0,
                    keepdims=True,
                )
                dq = None
                for kb in range(qb + 1):
                    keys = slice(kb * BLOCK, (kb + 1) * BLOCK)
                    at = starts[qb] + kb * BLOCK
                    p = probs[2 * g + a, at : at + BLOCK, :]
                    s_scr[0, kb, :, PAIR:] += mm(p, do)
                    dp = mm(qkv_ref[g, keys, 2 * PAIR :], do_t)
                    ds = (p.astype(F32) * (dp - dots)).astype(BF16)
                    s_scr[0, kb, :, :PAIR] += mm(ds, q)
                    part = mm(k_t[heads, keys], ds)
                    dq = part if dq is None else dq + part
                dq_parts.append(dq)
            dq_blocks.append(jnp.concatenate(dq_parts, axis=0) * (HALF**-0.5))
        for qb in range(nblk):
            rows = slice(qb * BLOCK, (qb + 1) * BLOCK)
            qkv_ref[g, rows, :] = jnp.concatenate([dq_blocks[qb].T, s_scr[0, qb]], axis=1).astype(BF16)
        put(g, 0, mm(x_t[...], qkv_ref[g]))
        return carry

    lax.fori_loop(0, pairs, attend_back, 0)

    if linked:
        for n in range(5):
            scatter_small.step(n, 0)
            for p in range(PIECES):
                scatter.step(n, p)

    def dx_copy(i):
        rows = slice(i * BLOCK, (i + 1) * BLOCK)
        return pltpu.make_async_copy(dx_ref.at[rows, :], dx_hbm.at[rows, :], out_sem.at[2, i])

    for qb in range(nblk):
        rows = slice(qb * BLOCK, (qb + 1) * BLOCK)
        total_dx = dx_ref[rows, :]
        for g in range(pairs):
            total_dx = total_dx + mm_nt(qkv_ref[g, rows, :], w_qkv(g))
        dx_ref[rows, :] = total_dx
        dx_copy(qb).start()

    for i in range(nblk):
        for cp in out_copies(pl.ds(i * BLOCK, BLOCK), i):
            cp.wait()
        dx_copy(i).wait()
    if linked:
        gather_small.step(5, 0)
        scatter_small.step(5, 0)
        for p in range(PIECES):
            gather.step(5, p)
            scatter.step(5, p)


def layer(linked, x_in, y_in, lengths, grad_x, grad_y, *rest):
    slots, width = x_in.shape
    ff = 4 * width
    nblk = slots // BLOCK
    pairs = H // 2
    causal = BLOCK * nblk * (nblk + 1) // 2
    vmem = pl.BlockSpec(memory_space=pltpu.VMEM)
    any_ = pl.BlockSpec(memory_space=pl.ANY)
    smem = pl.BlockSpec(memory_space=pltpu.SMEM)
    streams = (
        jax.ShapeDtypeStruct((slots, width), BF16),
        jax.ShapeDtypeStruct((slots, width), F32),
        jax.ShapeDtypeStruct((slots, width), F32),
    )
    wide = (PIECES,) + GRID + (ROWS, CHUNK)
    narrow = (1,) + GRID + (ROWS, PAIR)
    links = []
    if linked:
        outs = [jax.ShapeDtypeStruct(w.shape, F32) for w in rest]
        links += [pltpu.VMEM(wide, BF16), pltpu.VMEM(wide, BF16)]
        links += [pltpu.VMEM(narrow, BF16), pltpu.VMEM(narrow, BF16)]
        for n, _, _, _, _, r, lanes in (wide, narrow):
            links += [
                pltpu.VMEM((n, 4, 2, 2, r, lanes), BF16),
                pltpu.VMEM((n, 2, 4, r, lanes), BF16),
                pltpu.VMEM((n, 4, r, lanes), BF16),
                pltpu.VMEM((n, 3, r, lanes), BF16),
            ]
        for n in (PIECES, 1, PIECES, 1):
            links += [pltpu.SemaphoreType.DMA((n, Z + 3)), pltpu.SemaphoreType.DMA((n, Z + 3))]
        params = pltpu.CompilerParams(
            vmem_limit_bytes=VMEM_LIMIT, collective_id=0, has_side_effects=True
        )
    else:
        outs = [jax.ShapeDtypeStruct(wide, BF16), jax.ShapeDtypeStruct(narrow, BF16)]
        params = pltpu.CompilerParams(vmem_limit_bytes=VMEM_LIMIT)
    return pl.pallas_call(
        functools.partial(layer_kernel, linked),
        out_shape=streams + tuple(outs),
        in_specs=[smem] + [any_] * 4 + [vmem] * len(rest),
        out_specs=(any_,) * 3 + (vmem,) * len(outs),
        scratch_shapes=links
        + [
            pltpu.VMEM((slots, width), BF16),
            pltpu.VMEM((slots, width), F32),
            pltpu.VMEM((slots, width), BF16),
            pltpu.VMEM((slots, width), BF16),
            pltpu.VMEM((slots, width), F32),
            pltpu.VMEM((8, ff), F32),
            pltpu.VMEM((8, ff), F32),
            pltpu.VMEM((pairs, slots, 3 * PAIR), BF16),
            pltpu.VMEM((pairs, PAIR, slots), BF16),
            pltpu.VMEM((slots, width), BF16),
            pltpu.VMEM((pairs, PAIR, slots), BF16),
            pltpu.VMEM((H, causal, BLOCK), BF16),
            pltpu.VMEM((causal, BLOCK), F32),
            pltpu.VMEM((slots, ff), BF16),
            pltpu.VMEM((slots, ff), BF16),
            pltpu.VMEM((slots, width), BF16),
            pltpu.VMEM((slots, width), BF16),
            pltpu.VMEM((width, slots), BF16),
            pltpu.VMEM((2, nblk, BLOCK, BLOCK), F32),
            pltpu.SemaphoreType.DMA((4,)),
            pltpu.SemaphoreType.DMA((3, nblk)),
        ],
        compiler_params=params,
        name="layer",
    )(lengths, x_in, y_in, grad_x, grad_y, *rest)


BOTH = ("dp", "fsdp")


def on_device(
    linked,
    x_in,
    y_in,
    lengths,
    w_qkv,
    w_out,
    gain_one,
    bias_one,
    w_up,
    b_up,
    w_down,
    gain_two,
    bias_two,
    grad_x,
    grad_y,
):
    streams = (x_in, y_in, lengths, grad_x, grad_y)
    width = x_in.shape[1]
    if linked:
        small = jnp.concatenate([gain_one, bias_one, gain_two, bias_two, b_up])
        small = jnp.broadcast_to(small[None], (ROWS, small.shape[0]))
        x_out, y_out, d_x, d_qkv, d_out, d_up, d_down, d_small = layer(
            True, *streams, w_qkv, w_out, w_up, w_down, small
        )
        row = d_small[0]
        vectors = [row[n * ROWS : (n + 1) * ROWS] for n in range(4)] + [row[4 * ROWS :]]
    else:
        blocks = GRID[0] * GRID[1] * GRID[2] * GRID[3]
        pairs = H // 2

        def whole(w):
            return lax.all_gather(w, BOTH, axis=0, tiled=True)

        def cut(w):
            return w.reshape(GRID + (ROWS, CHUNK))

        qkv, out, up, down = (whole(w) for w in (w_qkv, w_out, w_up, w_down))
        pieces = []
        for g in range(pairs):
            lane = [slice(n * width + g * PAIR, n * width + (g + 1) * PAIR) for n in range(3)]
            pieces.append(cut(jnp.concatenate([qkv[:, s] for s in lane] + [out[:, lane[0]]], 1)))
        per = up.shape[1] // CHUNK
        pieces += [cut(up[:, j * CHUNK : (j + 1) * CHUNK]) for j in range(per)]
        down = down.reshape(blocks, per, ROWS, width)
        pieces += [cut(down[:, j].reshape(-1, width)) for j in range(per)]
        vectors = [whole(v) for v in (gain_one, bias_one, gain_two, bias_two, b_up)]
        small = jnp.concatenate([v.reshape(blocks, -1) for v in vectors], axis=1)
        small = jnp.broadcast_to(small[:, None], (blocks, ROWS, small.shape[1]))
        x_out, y_out, d_x, grads, d_small = layer(
            False, *streams, jnp.stack(pieces), small.reshape((1,) + GRID + (ROWS, -1))
        )

        def share(w):
            return lax.psum_scatter(w, BOTH, scatter_dimension=0, tiled=True)

        grads = grads.astype(F32).reshape(PIECES, -1, CHUNK)
        d_qkv = grads[:pairs, :, : 3 * PAIR].reshape(pairs, width, 3, PAIR)
        d_qkv = share(d_qkv.transpose(1, 2, 0, 3).reshape(width, 3 * width))
        d_out = share(grads[:pairs, :, 3 * PAIR :].transpose(1, 0, 2).reshape(width, width))
        d_up = share(grads[pairs : pairs + per].transpose(1, 0, 2).reshape(width, -1))
        d_down = grads[pairs + per :].reshape(per, blocks, ROWS, width).transpose(1, 0, 2, 3)
        d_down = share(d_down.reshape(-1, width))
        rows = d_small.astype(F32).reshape(blocks, ROWS, -1)[:, 0]
        vectors = [share(rows[:, n * ROWS : (n + 1) * ROWS].reshape(-1)) for n in range(4)]
        vectors.append(share(rows[:, 4 * ROWS :].reshape(-1)))
    return (
        x_out,
        y_out,
        d_x,
        d_qkv,
        d_out,
        vectors[0],
        vectors[1],
        d_up,
        vectors[4],
        d_down,
        vectors[2],
        vectors[3],
    )


def solution(mesh):
    matrix, vector = P(BOTH, None), P(BOTH)
    linked = mesh.shape["dp"] == Z and mesh.shape["fsdp"] == GRID[1] * GRID[2] * GRID[3]
    return jax.shard_map(
        functools.partial(on_device, linked),
        mesh=mesh,
        in_specs=(matrix,) * 5
        + (vector, vector, matrix, vector, matrix, vector, vector, matrix, matrix),
        out_specs=(matrix,) * 5
        + (vector, vector, matrix, vector, matrix, vector, vector),
        check_vma=False,
    )
```

time: 803 us -> 171 us (0.21); the launches traced: 794 us -> 171 us
  waiting for transfers between devices: 424 us -> 0 us
  Pallas kernels: 0 us -> 155 us
  matrix products: 145 us -> 0 us
  blocking collectives: 126 us -> 0 us
  other arithmetic: 37.1 us -> 0 us
  local copies, waits for them, and re-layouts: 45.3 us -> 15.4 us
  between operations: 15.1 us -> 0.68 us
    reduce_scatter x3 -> x0, waiting for transfers between devices: 313 us -> none  [the longest x1 143 us: on_device(): lax.psum_scatter(grad_up, ('dp', 'fsdp'), scatter_dimension=0, tiled=True)]
    pallas_call x0 -> x1, Pallas kernels: none -> 155 us  [layer(): pl.pallas_call(functools.partial(layer_kernel, linked), out_shape=streams...]
    dot_general x22 -> x0, matrix products: 124 us -> none  [the longest x2 21.4 us: on_device(): jnp.einsum('qhd,khd->hqk', grad_block, values_all, preferred_element_type...]
    unnamed x8 -> x0, waiting for transfers between devices: 107 us -> none
    unnamed x2 -> x0, blocking collectives: 81.1 us -> none
    all_gather x1 -> x0, blocking collectives: 44.8 us -> none  [on_device(): lax.all_gather(w_out, ('dp', 'fsdp'), axis=0, tiled=True)]
    convert_element_type x10 -> x0, other arithmetic: 28.9 us -> none  [the longest x2 23.2 us: on_device(): grad_scores = grad_scores.astype(jnp.bfloat16)]
    unnamed x121 -> x19, local copies, waits for them, and re-layouts: 34.5 us -> 8.52 us
  transfers between devices with their start and end apart: 7 -> 0, of which waited for: 5 -> 0; matrix products, arithmetic and copies ran while one was open for 18% -> 0% of each run, Pallas kernels for 0% -> 0%
where the time goes in v1:
time: 171 us
  Pallas kernels  155 us (91%)
  local copies, waits for them, and re-layouts  15.4 us (9%)
    pallas_call x1, Pallas kernels, layer(): pl.pallas_call(functools.partial(layer_kernel, linked), out_shape=streams...  155 us
    unnamed x19, local copies, waits for them, and re-layouts  8.52 us
    concatenate x1, local copies, waits for them, and re-layouts, on_device(): small = jnp.concatenate([gain_one, bias_one, gain_two, bias_two, b_up])  3.43 us

profile of v1, /device:TPU:0, one launch (start us, length us, event | category | flops | bytes accessed | tf_op | source)
XLA Modules:
  0.0 171.0 jit_solution(15419800797755968207)
XLA Ops:
  0.6 3.4 %concatenate.3 = bf16[128]{0:T(256)(128)(2,1)S(1)} concatenate(bf16[16]{0:T(256)(128)(2,1)} %param.19, bf16[16]{0:T(256)(128)(2,1)} %param.20, bf16[16]{0:T(256)(128)(2,1)} %param.24, bf16[16]{0:T(256)(128)(2,1)} %param.25, bf16[64]{0:T(256)(128)(2,1)} %param.22), dimensions={0} | concatenate | bytes 512 | tf_op jit(solution)/shard_map/concatenate | solution.py:700
  4.1 0.6 broadcast_in_dim.2.refs_9_
  4.7 155.0 %layer.1 = (bf16[1024,512]{1,0:T(8,128)(2,1)}, f32[1024,512]{1,0:T(8,128)}, f32[1024,512]{1,0:T(8,128)}, f32[16,1536]{1,0:T(8,128)}, f32[16,512]{1,0:T(8,128)}, ...) custom-call(s32[1,16]{1,0:T(1,128)} %refs_0_.1, bf16[1024,512]{1,0:T(8,128)(2,1)} %refs_1_.1, ...), custom_call_target="tpu_custom_call" | custom-call | tf_op jit(solution)/shard_map/layer/pallas_call | solution.py:643
  159.7 0.0 copy-start.1
  159.7 1.4 slice_bitcast_fusion.2
  161.1 1.4 slice_bitcast_fusion
  162.5 2.3 %copy.33 = bf16[1024,512]{1,0:T(8,128)(2,1)} copy(bf16[1024,512]{1,0:T(8,128)(2,1)} %get-tuple-element.44) | data formatting | bytes 2097152
  164.8 0.0 copy-done.1
  164.8 0.0 copy-start
  164.8 1.3 copy.34
  166.1 1.0 copy-done
  167.1 0.0 copy-start.4
  167.1 0.0 copy-start.5
  167.1 0.0 copy-start.3
  167.1 0.0 copy-start.2
  167.1 1.3 copy.35
  168.4 0.0 copy-done.4
  168.4 0.6 copy.36
  169.1 0.0 copy-done.5
  169.1 0.6 copy.37
  169.7 0.0 copy-done.3
  169.7 0.7 copy.38
  170.4 0.0 copy-done.2
  170.4 0.7 copy.39
Async XLA Ops:
  159.7 5.1 %copy-start.1 = (f32[1024,512]{1,0:T(8,128)S(1)}, f32[1024,512]{1,0:T(8,128)}, u32[]{:S(2)}) copy-start(f32[1024,512]{1,0:T(8,128)} %get-tuple-element.45) | copy-start | bytes 6291460
  164.8 2.3 %copy-start = (f32[1024,512]{1,0:T(8,128)S(1)}, f32[1024,512]{1,0:T(8,128)}, u32[]{:S(2)}) copy-start(f32[1024,512]{1,0:T(8,128)} %get-tuple-element.46) | copy-start | bytes 6291460
  167.1 1.3 copy-start.4
  167.1 2.0 %copy-start.5 = (f32[16,512]{1,0:T(8,128)S(1)}, f32[16,512]{1,0:T(8,128)}, u32[]{:S(2)}) copy-start(f32[16,512]{1,0:T(8,128)} %get-tuple-element.48) | copy-start | bytes 98308
  167.1 2.6 %copy-start.3 = (f32[16,2048]{1,0:T(8,128)S(1)}, f32[16,2048]{1,0:T(8,128)}, u32[]{:S(2)}) copy-start(f32[16,2048]{1,0:T(8,128)} %get-tuple-element.51) | copy-start | bytes 393220
  167.1 3.2 %copy-start.2 = (f32[64,512]{1,0:T(8,128)S(1)}, f32[64,512]{1,0:T(8,128)}, u32[]{:S(2)}) copy-start(f32[64,512]{1,0:T(8,128)} %get-tuple-element.53) | copy-start | bytes 393220

commit v2 on v1

--- a/solution.py
+++ b/solution.py
@@ -12,10 +12,13 @@
 HALF = 64
 BLOCK = 256
 CHUNK = 512
+SPAN = 128
 GRID = (4, 2, 2, 2)
 ROWS = 16
 Z = GRID[0]
 PIECES = 12
+FIRST_PIECE = 0
+LAST_PIECE = 3
 VMEM_LIMIT = 67000000
 EPSILON = 1e-05
 NEGATIVE = -1e30
@@ -36,6 +39,15 @@
 
 def mm_tn(a, b):
     return lax.dot_general(a, b, (((0,), (0,)), ((), ())), preferred_element_type=F32)
+
+
+def interleave(parts):
+    while parts:
+        for part in list(parts):
+            try:
+                next(part)
+            except StopIteration:
+                parts.remove(part)
 
 
 class Place:
@@ -89,13 +101,35 @@
         every = slice(None)
         return self.copy((p, every, every, every, c), a.device(a.z, a.y, a.x, 1 - a.c), p, Z + 2)
 
+    def straight(self, p):
+        return isinstance(p, int) and p == FIRST_PIECE and self.buf.shape[0] == PIECES
+
     def step(self, n, p):
         a = self.at
         y1, x1 = a.first(p)
         y2, x2 = a.second(p)
+        across = (1 - a.y, 1 - a.x)
         if n == 0:
             for d in range(1, Z):
                 self.along_z(p, d, a.z).start()
+        elif self.straight(p) and n in (1, 2, 3, 5):
+            if n == 1:
+                for d in range(1, Z):
+                    self.along_z(p, d, a.around(Z - d)).wait_recv()
+            trips = ((Z + 1, across), (Z - 1, (y1, x1)), (Z, (y2, x2)))
+            for k, to in trips:
+                if n == 1:
+                    self.plane(p, k, a.y, a.x, to).start()
+                elif n == 3:
+                    self.plane(p, k, to[0], to[1], to).wait_recv()
+                elif n == 5:
+                    self.plane(p, k, a.y, a.x, to).wait_send()
+            if n == 3:
+                self.core(p, a.c).start()
+            elif n == 5:
+                for d in range(1, Z):
+                    self.along_z(p, d, a.z).wait_send()
+                self.core(p, a.c).wait_send()
         elif n == 1:
             for d in range(1, Z):
                 self.along_z(p, d, a.around(Z - d)).wait_recv()
@@ -172,8 +206,31 @@
         y1, x1 = a.first(p)
         y2, x2 = a.second(p)
         every = slice(None)
+        across = (1 - a.y, 1 - a.x)
         if n == 0:
             self.core(p).start()
+        elif isinstance(p, int) and p == LAST_PIECE and n in (1, 2, 3, 5):
+            if n == 1:
+                self.core(p).wait_recv()
+                self.add((p, every, every, every, a.c), self.got_core[p])
+            for k, to in ((1, across), (2, (y1, x1)), (3, (y2, x2))):
+                if n == 1:
+                    self.plane(p, k, to[0], to[1], to).start()
+                elif n == 3:
+                    self.plane(p, k, to[0], to[1], to).wait_recv()
+                elif n == 5:
+                    self.plane(p, k, to[0], to[1], to).wait_send()
+            if n == 3:
+                total = self.buf[p, :, a.y, a.x, a.c].astype(F32) + self.got_first[p, 0].astype(F32)
+                total = total + self.got_first[p, 1].astype(F32) + self.got_second[p].astype(F32)
+                self.buf[p, :, a.y, a.x, a.c] = total.astype(BF16)
+            for d in range(1, Z):
+                if n == 3:
+                    self.along_z(p, d).start()
+                elif n == 5:
+                    self.along_z(p, d).wait_send()
+            if n == 5:
+                self.core(p).wait_send()
         elif n == 1:
             self.core(p).wait_recv()
             self.add((p, every, every, every, a.c), self.got_core[p])
@@ -205,6 +262,71 @@
                 self.along_z(p, d).wait_send()
 
 
+SMALL = "small"
+START_STEPS = (
+    ((False, 0, 0), (False, 0, 1), (False, SMALL, 0),),
+    (),
+    (),
+    (),
+    (),
+    ((False, 1, 0), (False, 2, 0), (False, 1, 1), (False, 0, 2), (False, 0, 3), (False, 1, 2), (False, 1, 3), (False, 0, 4), (False, 0, 5), (False, 3, 0),),
+)
+ATTEND_STEPS = (
+    (((False, 2, 1), (False, 4, 0),), (), ((False, SMALL, 1),), (), (), (),),
+    (((False, 1, 4), (False, 1, 5), (False, 2, 2), (False, 2, 3), (False, 0, 6), (False, 0, 7), (False, 3, 1), (False, 4, 1),), (), ((False, SMALL, 2),), (), (), (),),
+    (((False, 1, 6), (False, 2, 4), (False, 0, 8), (False, 2, 5), (False, 3, 2), (False, 3, 3), (False, 1, 7), (False, 0, 9), (False, 4, 2),), ((False, 4, 3),), ((False, SMALL, 3),), (), (), (),),
+    ((), ((False, 2, 6), (False, 1, 8), (False, 0, 10),), ((False, 3, 4), (False, 3, 5), (False, 2, 7),), ((False, 1, 9), (False, 0, 11),), (), ((False, 4, 4), (False, 4, 5),),),
+)
+AFTER_ATTEND = ((False, SMALL, 4),)
+NORM_STEPS = (
+    ((),),
+    (((False, 2, 8), (False, 1, 10),),),
+    ((),),
+    (((False, 3, 6), (False, 1, 11),),),
+)
+AFTER_NORM = ((False, 3, 7), (False, 2, 9), (False, 4, 6), (False, 4, 7),)
+UP_STEPS = (
+    (((False, 2, 10),),),
+    ((),),
+    (((False, 3, 8),),),
+    (((False, 3, 9), (False, 2, 11),),),
+)
+AFTER_UP = ((False, 4, 8), (False, 3, 10), (False, 4, 9), (False, 4, 10), (False, 3, 11), (False, 4, 11),)
+AFTER_DOWN = ((True, 0, 0), (True, 0, 1), (True, 0, 2), (True, 0, 3),)
+BACK_STEPS = (
+    ((), (), (),),
+    (((True, 1, 0), (True, 1, 1), (True, 1, 2),), ((True, 1, 3),), (),),
+    ((), (), (),),
+    ((), (), ((True, 2, 0), (True, 2, 1), (True, 2, 2),),),
+)
+UP_SUM_STEPS = (
+    ((True, 2, 3), (True, 0, 4),),
+    ((True, 0, 5),),
+    ((True, 1, 4), (True, 0, 6),),
+    ((True, 3, 0), (True, 3, 1), (True, 1, 5), (True, 3, 2),),
+)
+OUT_SUM_STEPS = ((True, SMALL, 0), (True, 3, 3), (True, 1, 6), (True, 0, 7),)
+ATTEND_BACK_STEPS = (
+    ((), ((True, 2, 4), (True, 1, 7),), ((True, 2, 5),), ((True, 4, 0), (True, SMALL, 1),), ((True, 4, 1), (True, 2, 6), (True, 4, 2),), ((True, 4, 3), (True, 0, 8),),),
+    ((), ((True, 3, 4), (True, 3, 5), (True, 1, 8),), ((True, 2, 7), (True, 3, 6),), ((True, SMALL, 2),), (), ((True, 0, 9),),),
+    ((), ((True, 4, 4), (True, 1, 9), (True, 4, 5),), ((True, 4, 6), (True, 3, 7), (True, 2, 8),), ((True, SMALL, 3),), (), ((True, 0, 10),),),
+    ((), ((True, 1, 10), (True, 4, 7), (True, 2, 9),), ((True, 3, 8),), ((True, SMALL, 4),), (), ((True, 0, 11),),),
+)
+INPUT_STEPS = (
+    (),
+    ((True, 1, 11),),
+    ((True, 4, 8), (True, 3, 9), (True, 2, 10),),
+    ((True, 2, 11),),
+)
+LAST_STEPS = ((True, 4, 9), (True, 3, 10), (True, 3, 11), (True, 4, 10), (True, 4, 11),)
+
+
+def piece_at(order):
+    if isinstance(order, int):
+        return (8, 4, 0)[order // 4] + order % 4
+    return jnp.where(order < 4, order + 8, jnp.where(order < 8, order, order - 8))
+
+
 def as_matrix(value):
     return value.reshape(-1, value.shape[-1])
 
@@ -219,8 +341,9 @@
 
     lengths_ref, x_hbm, y_hbm, gx_hbm, gy_hbm = take(5)
     if linked:
-        s_qkv, s_out, s_up, s_down, s_small = take(5)
-        xo_hbm, yo_hbm, dx_hbm, o_qkv, o_out, o_up, o_down, o_small = take(8)
+        s_qkv, s_out, s_up, s_down = take(4)
+        vectors = take(5)
+        xo_hbm, yo_hbm, dx_hbm, shares, o_small = take(5)
         weights, grads, small, g_small = take(4)
         got = take(8)
         sems = take(8)
@@ -235,9 +358,10 @@
         dx_ref,
         params,
         sums,
-        qkv_ref,
+        kv_ref,
+        q_t,
         att_t,
-        datt,
+        inverses,
         datt_t,
         probs,
         bias,
@@ -273,6 +397,7 @@
             place.device(z, y, x, 1 - c),
             place.device(z, y, 1 - x, c),
             place.device(z, 1 - y, x, c),
+            place.device(z, 1 - y, 1 - x, c),
         ] + [place.device(place.around(d), y, x, c) for d in range(1, Z)]
         for partner in partners:
             pl.semaphore_signal(barrier, inc=1, device_id=partner, device_id_type=MESH)
@@ -283,21 +408,19 @@
         for j in range(per):
             weights[pairs + j, z, y, x, c] = s_up[:, j * CHUNK : (j + 1) * CHUNK]
             weights[pairs + per + j, z, y, x, c] = s_down[j * ROWS : (j + 1) * ROWS, :]
-        small[0, z, y, x, c] = s_small[...]
+        packed = jnp.zeros((ROWS, PAIR), F32)
+        at = 0
+        for ref in vectors:
+            r = ref.shape[0]
+            row = jnp.broadcast_to(ref[...].astype(F32).reshape(1, r), (ROWS, r)).astype(BF16)
+            column = lax.broadcasted_iota(jnp.int32, (r, PAIR), 1)
+            packed += mm(row, (column == lax.broadcasted_iota(jnp.int32, (r, PAIR), 0) + at).astype(BF16))
+            at += r
+        small[0, z, y, x, c] = packed.astype(BF16)
         pl.semaphore_wait(barrier, len(partners))
 
         def finish(p, total):
-            if isinstance(p, int):
-                if p < pairs:
-                    for n in range(3):
-                        lane = slice(n * width + p * PAIR, n * width + (p + 1) * PAIR)
-                        o_qkv[:, lane] = total[:, n * PAIR : (n + 1) * PAIR]
-                    o_out[:, p * PAIR : (p + 1) * PAIR] = total[:, 3 * PAIR :]
-                elif p < pairs + per:
-                    o_up[:, (p - pairs) * CHUNK : (p - pairs + 1) * CHUNK] = total
-                else:
-                    at = (p - pairs - per) * ROWS
-                    o_down[at : at + ROWS, :] = total
+            shares[p] = total
 
         def finish_small(p, total):
             o_small[...] = total
@@ -306,10 +429,46 @@
         gather_small = Gather(place, small, sems[2], sems[3])
         scatter = Scatter(place, grads, *got[:4], sems[4], sems[5], finish)
         scatter_small = Scatter(place, g_small, *got[4:], sems[6], sems[7], finish_small)
-        for n in range(5):
-            gather_small.step(n, 0)
-            for p in range(PIECES):
-                gather.step(n, p)
+    def run_step(scattered, n, order):
+        if scattered:
+            scatter.step(n, piece_at(order))
+        else:
+            gather.step(n, order)
+
+    def steps(events):
+        if linked:
+            for event in events:
+                if event[1] == SMALL:
+                    (scatter_small if event[0] else gather_small).step(event[2], 0)
+                else:
+                    run_step(*event)
+
+    def steps_in_loop(i, table, slot):
+        if not linked:
+            return
+        kinds = []
+        for row in table:
+            for event in row[slot]:
+                if event[1] != SMALL and event[:2] not in kinds:
+                    kinds.append(event[:2])
+        kinds.sort(key=lambda kind: kind[1])
+        for kind in kinds:
+            columns = [[e[2] for e in row[slot] if e[:2] == kind] for row in table]
+            for k in range(max(len(column) for column in columns)):
+                have = [j for j, column in enumerate(columns) if len(column) > k]
+                order = jnp.int32(columns[have[0]][k])
+                wanted = i == have[0]
+                for j in have[1:]:
+                    order = jnp.where(i == j, columns[j][k], order)
+                    wanted = wanted | (i == j)
+                if len(have) == len(columns):
+                    run_step(*kind, order)
+                else:
+                    pl.when(wanted)(functools.partial(run_step, *kind, order))
+        for j, row in enumerate(table):
+            for e in row[slot]:
+                if e[1] == SMALL:
+                    pl.when(i == j)(functools.partial(steps, (e,)))
 
     def segments(pos):
         seg = jnp.zeros(pos.shape, jnp.int32)
@@ -320,6 +479,7 @@
         return jnp.where(pos < end, seg, -1 - pos), end
 
     starts = [BLOCK * (qb * (qb + 1) // 2) for qb in range(nblk)]
+    steps(START_STEPS[0])
     for qb in range(nblk):
         q_pos = lax.broadcasted_iota(jnp.int32, (1, BLOCK), 1) + qb * BLOCK
         q_seg, total = segments(q_pos)
@@ -331,6 +491,7 @@
                 allowed = allowed & (k_pos <= q_pos)
             at = starts[qb] + kb * BLOCK
             bias[at : at + BLOCK, :] = jnp.where(allowed, 0.0, NEGATIVE).astype(F32)
+        steps(START_STEPS[1 + qb])
 
     loads[0].wait()
     x_t[...] = x_ref[...].T
@@ -342,6 +503,108 @@
         own = lax.broadcasted_iota(jnp.int32, (rows, width), 0)
         mine = own == (lax.broadcasted_iota(jnp.int32, (rows, width), 1) // r) * ROWS
         return jnp.sum(jnp.where(mine, mm(first, pick), 0.0), axis=0, keepdims=True)
+
+    def w_qkv(g):
+        return as_matrix(weights[g, ..., : 3 * PAIR])
+
+    def w_out():
+        return jnp.concatenate(
+            [as_matrix(weights[g, ..., 3 * PAIR :]) for g in range(pairs)], axis=1
+        )
+
+    def w_up(j):
+        return as_matrix(weights[pairs + j])
+
+    def w_down(j):
+        parts = [weights[pairs + per + n, j].reshape(-1, ROWS, width) for n in range(per)]
+        return as_matrix(jnp.stack(parts, axis=1))
+
+    steps(START_STEPS[1 + nblk])
+
+    def across(kb, qb):
+        at = BLOCK * (kb * nblk - kb * (kb - 1) // 2 + qb - kb)
+        return slice(at, at + BLOCK)
+
+    def seen_by(kb):
+        return slice(across(kb, kb).start, across(kb, nblk - 1).stop)
+
+    def half_rows(value, a):
+        own = value[a * HALF : (a + 1) * HALF]
+        rest = jnp.zeros_like(own)
+        return jnp.concatenate([rest, own] if a else [own, rest], axis=0)
+
+    def attend(g, carry):
+        steps_in_loop(g, ATTEND_STEPS, 0)
+        weights_g = w_qkv(g)
+        for qb in range(nblk):
+            rows = slice(qb * BLOCK, (qb + 1) * BLOCK)
+            kv_ref[g, rows, :] = mm(x_ref[rows, :], weights_g[:, PAIR:]).astype(BF16)
+        q = mm_tn(weights_g[:, :PAIR], x_t[...]).astype(BF16).astype(F32)
+        q_t[g] = (q * (HALF**-0.5)).astype(BF16)
+        v_t = kv_ref[g, :, PAIR:].T
+        steps_in_loop(g, ATTEND_STEPS, 1)
+
+        def scores(unit, buf):
+            qb, a = unit
+            nk = (qb + 1) * BLOCK
+            part = mm(kv_ref[g, :nk, :PAIR], half_rows(q_t[g, :, qb * BLOCK : nk], a))
+            s_scr[buf, : qb + 1] = part.reshape(qb + 1, BLOCK, BLOCK)
+            yield
+
+        def masked(unit, buf, r):
+            at = starts[unit[0]] + r
+            return s_scr[buf, r // BLOCK, r % BLOCK : r % BLOCK + SPAN] + bias[at : at + SPAN, :]
+
+        def soften(unit, buf):
+            qb, a = unit
+            top = None
+            for r in range(0, (qb + 1) * BLOCK, SPAN):
+                high = jnp.max(masked(unit, buf, r).reshape(-1, 8, BLOCK), axis=0)
+                top = high if top is None else jnp.maximum(top, high)
+                yield
+            top = jnp.max(top, axis=0, keepdims=True)
+            whole = None
+            for r in range(0, (qb + 1) * BLOCK, SPAN):
+                e = jnp.exp(masked(unit, buf, r) - top)
+                one = jnp.sum(e.reshape(-1, 8, BLOCK), axis=0)
+                whole = one if whole is None else whole + one
+                lanes = across(r // BLOCK, qb)
+                probs[2 * g + a, r % BLOCK : r % BLOCK + SPAN, lanes] = e.astype(BF16)
+                yield
+            whole = jnp.sum(whole, axis=0, keepdims=True)
+            inverses[2 * g + a, :, qb * BLOCK : (qb + 1) * BLOCK] = 1.0 / whole
+
+        def mix(unit):
+            qb, a = unit
+            rows = slice(qb * BLOCK, (qb + 1) * BLOCK)
+            heads = slice(a * HALF, (a + 1) * HALF)
+            out = None
+            for kb in range(qb + 1):
+                keys = slice(kb * BLOCK, (kb + 1) * BLOCK)
+                part = mm(v_t[heads, keys], probs[2 * g + a, :, across(kb, qb)])
+                out = part if out is None else out + part
+                yield
+            att_t[g, heads, rows] = (out * inverses[2 * g + a, :, rows]).astype(BF16)
+
+        units = [(qb, a) for qb in range(nblk) for a in range(2)]
+        for t in range(len(units) + 2):
+            parts = []
+            if t < len(units):
+                parts.append(scores(units[t], t % 2))
+            if 1 <= t <= len(units):
+                parts.append(soften(units[t - 1], (t - 1) % 2))
+            if t >= 2:
+                parts.append(mix(units[t - 2]))
+            interleave(parts)
+            if t % 2 and t > 1:
+                steps_in_loop(g, ATTEND_STEPS, 1 + t // 2)
+        return carry
+
+    lax.fori_loop(0, pairs, attend, 0)
+
+    steps(AFTER_ATTEND)
+    for cp in loads[1:]:
+        cp.wait()
 
     blocks = as_matrix(small[0])
     for n in range(4):
@@ -352,69 +615,6 @@
             blocks[j * rows : (j + 1) * rows], 4 * ROWS, ff * ROWS // width
         )
 
-    lane = lax.broadcasted_iota(jnp.int32, (BLOCK, PAIR), 1)
-    sub = lax.broadcasted_iota(jnp.int32, (PAIR, BLOCK), 0)
-
-    def one_head(index, value, a):
-        keep = index < HALF if a == 0 else index >= HALF
-        return jnp.where(keep, value.astype(F32), 0.0).astype(BF16)
-
-    def w_qkv(g):
-        return as_matrix(weights[g, ..., : 3 * PAIR])
-
-    def w_out():
-        return jnp.concatenate(
-            [as_matrix(weights[g, ..., 3 * PAIR :]) for g in range(pairs)], axis=1
-        )
-
-    def w_up(j):
-        return as_matrix(weights[pairs + j])
-
-    def w_down(j):
-        parts = [weights[pairs + per + n, j].reshape(-1, ROWS, width) for n in range(per)]
-        return as_matrix(jnp.stack(parts, axis=1))
-
-    def attend(g, carry):
-        for qb in range(nblk):
-            rows = slice(qb * BLOCK, (qb + 1) * BLOCK)
-            part = mm(x_ref[rows, :], w_qkv(g))
-            q = part[:, :PAIR].astype(BF16).astype(F32) * (HALF**-0.5)
-            qkv_ref[g, rows, :] = jnp.concatenate([q, part[:, PAIR:]], axis=1).astype(BF16)
-        v_t = qkv_ref[g, :, 2 * PAIR :].T
-        for qb in range(nblk):
-            for a in range(2):
-                rows = slice(qb * BLOCK, (qb + 1) * BLOCK)
-                q = one_head(lane, qkv_ref[g, rows, :PAIR], a)
-                top = None
-                for kb in range(qb + 1):
-                    k = qkv_ref[g, kb * BLOCK : (kb + 1) * BLOCK, PAIR : 2 * PAIR]
-                    at = starts[qb] + kb * BLOCK
-                    s = mm_nt(k, q) + bias[at : at + BLOCK, :]
-                    s_scr[a, kb] = s
-                    high = jnp.max(s, axis=0, keepdims=True)
-                    top = high if top is None else jnp.maximum(top, high)
-                whole = None
-                for kb in range(qb + 1):
-                    e = jnp.exp(s_scr[a, kb] - top)
-                    s_scr[a, kb] = e
-                    one = jnp.sum(e, axis=0, keepdims=True)
-                    whole = one if whole is None else whole + one
-                inverse = 1.0 / whole
-                out = None
-                for kb in range(qb + 1):
-                    at = starts[qb] + kb * BLOCK
-                    p = (s_scr[a, kb] * inverse).astype(BF16)
-                    probs[2 * g + a, at : at + BLOCK, :] = p
-                    o = mm(v_t[a * HALF : (a + 1) * HALF, kb * BLOCK : (kb + 1) * BLOCK], p)
-                    out = o if out is None else out + o
-                att_t[g, a * HALF : (a + 1) * HALF, rows] = out.astype(BF16)
-        return carry
-
-    lax.fori_loop(0, pairs, attend, 0)
-
-    for cp in loads[1:]:
-        cp.wait()
-
     sums[...] = jnp.zeros_like(sums)
     gain_one = params[0:1, :width]
     bias_one = params[1:2, :width]
@@ -443,64 +643,111 @@
             pltpu.make_async_copy(y_buf.at[rows, :], yo_hbm.at[rows, :], out_sem.at[1, i]),
         )
 
-    def slab(j, n):
-        return divmod(j * (CHUNK // BLOCK) + n, nblk)
-
-    def rows_of_tile(i, carry):
-        r0 = pl.multiple_of(i * BLOCK, BLOCK)
-        rows = pl.ds(r0, BLOCK)
+    def keep_norm(i, value, inv):
+        for n in range(width // BLOCK):
+            bias[pl.ds(n * slots + i * BLOCK, BLOCK), :] = value[:, n * BLOCK : (n + 1) * BLOCK]
+        wide = jnp.broadcast_to(inv, (BLOCK, PAIR))
+        at = pl.multiple_of(width // BLOCK * slots + i * PAIR, PAIR)
+        bias[pl.ds(at, PAIR), :PAIR] = wide[:PAIR]
+        bias[pl.ds(at, PAIR), PAIR:] = wide[PAIR:]
+
+    def kept_norm(i):
+        value = [bias[pl.ds(n * slots + i * BLOCK, BLOCK), :] for n in range(width // BLOCK)]
+        at = pl.multiple_of(width // BLOCK * slots + i * PAIR, PAIR)
+        inv = [bias[pl.ds(at, PAIR), n * PAIR : n * PAIR + 1] for n in range(BLOCK // PAIR)]
+        return jnp.concatenate(value, axis=1), jnp.concatenate(inv, axis=0)
+
+    def first_norm_rows(i, carry):
+        rows = pl.ds(pl.multiple_of(i * BLOCK, BLOCK), BLOCK)
         at_tile = att_t[:, :, rows].reshape(width, BLOCK).T
         branch_a = mm(at_tile, w_out())
         n1, inv1 = norm(x_ref[rows, :].astype(F32) + branch_a)
-        x_mid = n1 * gain_one + bias_one
-        xl = x_mid.astype(BF16)
-        x_low[rows, :] = xl
-        branch_f = None
+        keep_norm(i, n1, inv1)
+        x_low[rows, :] = (n1 * gain_one + bias_one).astype(BF16)
+        y_buf[rows, :] += branch_a
+        steps_in_loop(i, NORM_STEPS, 0)
+        return carry
+
+    lax.fori_loop(0, nblk, first_norm_rows, 0)
+    steps(AFTER_NORM)
+
+    def up_rows(i, carry):
+        rows = pl.ds(pl.multiple_of(i * BLOCK, BLOCK), BLOCK)
+        xl = x_low[rows, :]
         for j in range(per):
             cols = slice(j * CHUNK, (j + 1) * CHUNK)
             u = mm(xl, w_up(j)) + params[4:5, cols]
             u2 = u * u
             t = jnp.tanh(u * (GELU_C + (GELU_C * GELU_K) * u2))
             h = 0.5 + 0.5 * t
-            low = (u * h).astype(BF16)
-            hidden[rows, cols] = low
+            hidden[rows, cols] = (u * h).astype(BF16)
             slope = h + h * (1.0 - h) * (u * (2.0 * GELU_C + (6.0 * GELU_C * GELU_K) * u2))
-            for n in range(CHUNK // BLOCK):
-                s_scr[slab(j, n)] = slope[:, n * BLOCK : (n + 1) * BLOCK]
-            part = mm(low, w_down(j))
+            du_ref[rows, cols] = slope.astype(BF16)
+        steps_in_loop(i, UP_STEPS, 0)
+        return carry
+
+    lax.fori_loop(0, nblk, up_rows, 0)
+    steps(AFTER_UP)
+
+    def down_rows(i, carry):
+        r0 = pl.multiple_of(i * BLOCK, BLOCK)
+        rows = pl.ds(r0, BLOCK)
+        branch_f = None
+        for j in range(per):
+            part = mm(hidden[rows, j * CHUNK : (j + 1) * CHUNK], w_down(j))
             branch_f = part if branch_f is None else branch_f + part
+        x_mid = kept_norm(i)[0] * gain_one + bias_one
         n2, inv2 = norm(x_mid + branch_f)
         live = (lax.broadcasted_iota(jnp.int32, (BLOCK, width), 0) + r0) < total
         gx = jnp.where(live, gx_buf[rows, :].astype(F32), 0.0)
         gy = jnp.where(live, gy_buf[rows, :].astype(F32), 0.0)
         gx_buf[rows, :] = jnp.where(live, n2 * gain_two + bias_two, 0.0).astype(BF16)
-        y_buf[rows, :] = jnp.where(live, y_buf[rows, :] + branch_a + branch_f, 0.0)
+        y_buf[rows, :] = jnp.where(live, y_buf[rows, :] + branch_f, 0.0)
         for cp in out_copies(rows, i):
             cp.start()
         add_sum(3, 0, gx)
         add_sum(2, 0, gx * n2)
         dr2 = norm_back(gx, gain_two, n2, inv2)
-        df = (dr2 + gy).astype(BF16)
-        df_ref[rows, :] = df
-        dx_mid = dr2
+        dx_ref[rows, :] = dr2
+        df_ref[rows, :] = (dr2 + gy).astype(BF16)
+        return carry
+
+    lax.fori_loop(0, nblk, down_rows, 0)
+
+    for j in range(per):
+        part = mm_tn(hidden[:, j * CHUNK : (j + 1) * CHUNK], df_ref[...]).astype(BF16)
+        part = part.reshape(-1, per, ROWS, width)
+        for n in range(per):
+            grads[pairs + per + n, j] = part[:, n].reshape(GRID[1:] + (ROWS, width))
+    steps(AFTER_DOWN)
+
+    def backward_rows(i, carry):
+        r0 = pl.multiple_of(i * BLOCK, BLOCK)
+        rows = pl.ds(r0, BLOCK)
+        df = df_ref[rows, :]
+        dx_mid = dx_ref[rows, :]
         for j in range(per):
             cols = slice(j * CHUNK, (j + 1) * CHUNK)
-            slope = jnp.concatenate([s_scr[slab(j, n)] for n in range(CHUNK // BLOCK)], axis=1)
-            du = (mm_nt(df, w_down(j)) * slope).astype(BF16)
+            du = (mm_nt(df, w_down(j)) * du_ref[rows, cols].astype(F32)).astype(BF16)
             du_ref[rows, cols] = du
             add_sum(4, j * CHUNK, du.astype(F32))
             dx_mid = dx_mid + mm_nt(du, w_up(j))
+            if j % 2:
+                steps_in_loop(i, BACK_STEPS, j // 2)
+        n1, inv1 = kept_norm(i)
+        live = (lax.broadcasted_iota(jnp.int32, (BLOCK, width), 0) + r0) < total
+        gy = jnp.where(live, gy_buf[rows, :].astype(F32), 0.0)
         add_sum(1, 0, dx_mid)
         add_sum(0, 0, dx_mid * n1)
         dr1 = norm_back(dx_mid, gain_one, n1, inv1)
         dx_ref[rows, :] = dr1
         da = (dr1 + gy).astype(BF16)
         gy_buf[rows, :] = da
-        datt[rows, :] = mm_nt(da, w_out()).astype(BF16)
         datt_t[:, :, rows] = mm_nt(w_out(), da).astype(BF16).reshape(pairs, PAIR, BLOCK)
+        steps_in_loop(i, BACK_STEPS, 2)
         return carry
 
-    lax.fori_loop(0, nblk, rows_of_tile, 0)
+    lax.fori_loop(0, nblk, backward_rows, 0)
 
     def put(p, at, value):
         grads[p, ..., at : at + value.shape[1]] = value.astype(BF16).reshape(
@@ -508,12 +755,8 @@
         )
 
     for j in range(per):
-        part = mm_tn(hidden[:, j * CHUNK : (j + 1) * CHUNK], df_ref[...]).astype(BF16)
-        part = part.reshape(-1, per, ROWS, width)
-        for n in range(per):
-            grads[pairs + per + n, j] = part[:, n].reshape(GRID[1:] + (ROWS, width))
-    for j in range(per):
         put(pairs + j, 0, mm_tn(x_low[...], du_ref[:, j * CHUNK : (j + 1) * CHUNK]))
+        steps(UP_SUM_STEPS[j])
     part = mm(att_t[...].reshape(width, slots), gy_buf[...])
     for g in range(pairs):
         put(g, 3 * PAIR, part[:, g * PAIR : (g + 1) * PAIR])
@@ -535,50 +778,115 @@
         rest = rest + gathered(sums[n : n + 1, :width], n * ROWS, ROWS)
     g_small[0] = rest.astype(BF16).reshape(GRID + (ROWS, PAIR))
 
+    steps(OUT_SUM_STEPS)
+
+    def ds_at(a, kb, qb=None):
+        at = (0, nblk, 0, nblk - 2)[kb] * BLOCK
+        lanes = slice(at, at + (nblk - kb) * BLOCK)
+        if qb is not None:
+            lanes = slice(at + (qb - kb) * BLOCK, at + (qb - kb + 1) * BLOCK)
+        row = (2 * a + kb // 2) * BLOCK
+        return slice(row, row + BLOCK), lanes
+
+    def grads_of(g):
+        return pl.ds(pl.multiple_of(g * 3 * PAIR, PAIR), 3 * PAIR)
+
+    def own_lanes(n, a):
+        at = 3 * width + (2 * n + a) * PAIR
+        return slice(at, at + PAIR)
+
+    lane = lax.broadcasted_iota(jnp.int32, (slots, PAIR), 1)
+
+    def put_halves(n, value):
+        value = value.astype(F32)
+        du_ref[:, own_lanes(n, 0)] = jnp.where(lane < HALF, value, 0.0).astype(BF16)
+        du_ref[:, own_lanes(n, 1)] = jnp.where(lane < HALF, 0.0, value).astype(BF16)
+
+    turned = slice(slots, 2 * slots)
+    key_rows, do_rows = BLOCK, BLOCK + PAIR
+
     def attend_back(g, carry):
-        k_t = qkv_ref[g, :, PAIR : 2 * PAIR].T
-        s_scr[0] = jnp.zeros((nblk, BLOCK, BLOCK), F32)
-        lanes = pl.ds(pl.multiple_of(g * PAIR, PAIR), PAIR)
-        dq_blocks = []
-        for qb in range(nblk):
-            rows = slice(qb * BLOCK, (qb + 1) * BLOCK)
-            dq_parts = []
-            for a in range(2):
-                heads = slice(a * HALF, (a + 1) * HALF)
-                q = one_head(lane, qkv_ref[g, rows, :PAIR], a)
-                do = one_head(lane, datt[rows, lanes], a)
-                do_t = one_head(sub, datt_t[g, :, rows], a)
-                dots = jnp.sum(
-                    att_t[g, heads, rows].astype(F32) * datt_t[g, heads, rows].astype(F32),
-                    axis=0,
-                    keepdims=True,
-                )
-                dq = None
-                for kb in range(qb + 1):
-                    keys = slice(kb * BLOCK, (kb + 1) * BLOCK)
-                    at = starts[qb] + kb * BLOCK
-                    p = probs[2 * g + a, at : at + BLOCK, :]
-                    s_scr[0, kb, :, PAIR:] += mm(p, do)
-                    dp = mm(qkv_ref[g, keys, 2 * PAIR :], do_t)
-                    ds = (p.astype(F32) * (dp - dots)).astype(BF16)
-                    s_scr[0, kb, :, :PAIR] += mm(ds, q)
-                    part = mm(k_t[heads, keys], ds)
-                    dq = part if dq is None else dq + part
-                dq_parts.append(dq)
-            dq_blocks.append(jnp.concatenate(dq_parts, axis=0) * (HALF**-0.5))
-        for qb in range(nblk):
-            rows = slice(qb * BLOCK, (qb + 1) * BLOCK)
-            qkv_ref[g, rows, :] = jnp.concatenate([dq_blocks[qb].T, s_scr[0, qb]], axis=1).astype(BF16)
-        put(g, 0, mm(x_t[...], qkv_ref[g]))
+        def put_grad(n, block, value):
+            rows = slice(block * BLOCK, (block + 1) * BLOCK)
+            lanes = pl.ds(pl.multiple_of(g * 3 * PAIR + n * PAIR, PAIR), PAIR)
+            du_ref[rows, lanes] = value.astype(BF16)
+
+        hidden[key_rows : key_rows + PAIR, turned] = kv_ref[g, :, :PAIR].T
+        for a in range(2):
+            heads = slice(a * HALF, (a + 1) * HALF)
+            scaled = datt_t[g, heads, :].astype(F32) * inverses[2 * g + a]
+            dots = jnp.sum(att_t[g, heads, :].astype(F32) * scaled, axis=0, keepdims=True)
+            inverses[2 * g + a] = dots
+            hidden[do_rows + a * HALF : do_rows + (a + 1) * HALF, turned] = scaled.astype(BF16)
+        put_halves(0, hidden[do_rows : do_rows + PAIR, turned].T)
+        put_halves(1, q_t[g].T)
+        steps_in_loop(g, ATTEND_BACK_STEPS, 0)
+
+        def through_values(unit, buf):
+            qb, a = unit
+            nk = (qb + 1) * BLOCK
+            do = half_rows(hidden[do_rows : do_rows + PAIR, slots + qb * BLOCK : slots + nk], a)
+            s_scr[buf, : qb + 1] = mm(kv_ref[g, :nk, PAIR:], do).reshape(qb + 1, BLOCK, BLOCK)
+            yield
+
+        def through_softmax(unit, buf):
+            qb, a = unit
+            dots = inverses[2 * g + a, :, qb * BLOCK : (qb + 1) * BLOCK]
+            for r in range(0, (qb + 1) * BLOCK, SPAN):
+                inner = slice(r % BLOCK, r % BLOCK + SPAN)
+                p = probs[2 * g + a, inner, across(r // BLOCK, qb)].astype(F32)
+                rows, lanes = ds_at(a, r // BLOCK, qb)
+                ds = p * (s_scr[buf, r // BLOCK, inner] - dots)
+                hidden[rows.start + r % BLOCK : rows.start + r % BLOCK + SPAN, lanes] = ds.astype(BF16)
+                yield
+
+        def to_queries(unit, kept):
+            qb, a = unit
+            out = None
+            for kb in range(qb + 1):
+                keys = slice(slots + kb * BLOCK, slots + (kb + 1) * BLOCK)
+                k = hidden[key_rows + a * HALF : key_rows + (a + 1) * HALF, keys]
+                part = mm(k, hidden[ds_at(a, kb, qb)])
+                out = part if out is None else out + part
+                yield
+            kept[unit] = out * (HALF**-0.5)
+            if a:
+                put_grad(0, qb, jnp.concatenate([kept[qb, 0], kept[qb, 1]], axis=0).T)
+
+        def to_values(unit, kept):
+            kb, a = unit
+            kept[unit] = mm(probs[2 * g + a, :, seen_by(kb)], du_ref[kb * BLOCK :, own_lanes(0, a)])
+            yield
+            if a:
+                put_grad(2, kb, kept[kb, 0] + kept[kb, 1])
+
+        def to_keys(unit, kept):
+            kb, a = unit
+            kept[unit] = mm(hidden[ds_at(a, kb)], du_ref[kb * BLOCK :, own_lanes(1, a)])
+            yield
+            if a:
+                put_grad(1, kb, kept[kb, 0] + kept[kb, 1])
+
+        kept = {}, {}, {}
+        units = [(qb, a) for qb in reversed(range(nblk)) for a in range(2)]
+        for t in range(len(units) + 2):
+            parts = []
+            if t < len(units):
+                parts.append(through_values(units[t], t % 2))
+                parts.append(to_values(units[t], kept[0]))
+            if 1 <= t <= len(units):
+                parts.append(through_softmax(units[t - 1], (t - 1) % 2))
+            if t >= 2:
+                parts.append(to_queries(units[t - 2], kept[1]))
+                parts.append(to_keys(units[t - 2], kept[2]))
+            interleave(parts)
+            if t % 2 and t > 1:
+                steps_in_loop(g, ATTEND_BACK_STEPS, t // 2)
+        put(g, 0, mm(x_t[...], du_ref[:, grads_of(g)]))
+        steps_in_loop(g, ATTEND_BACK_STEPS, 1 + nblk)
         return carry
 
     lax.fori_loop(0, pairs, attend_back, 0)
-
-    if linked:
-        for n in range(5):
-            scatter_small.step(n, 0)
-            for p in range(PIECES):
-                scatter.step(n, p)
 
     def dx_copy(i):
         rows = slice(i * BLOCK, (i + 1) * BLOCK)
@@ -588,10 +896,12 @@
         rows = slice(qb * BLOCK, (qb + 1) * BLOCK)
         total_dx = dx_ref[rows, :]
         for g in range(pairs):
-            total_dx = total_dx + mm_nt(qkv_ref[g, rows, :], w_qkv(g))
+            grad = du_ref[rows, g * 3 * PAIR : (g + 1) * 3 * PAIR]
+            total_dx = total_dx + mm_nt(grad, w_qkv(g))
         dx_ref[rows, :] = total_dx
         dx_copy(qb).start()
-
+        steps(INPUT_STEPS[qb])
+    steps(LAST_STEPS)
     for i in range(nblk):
         for cp in out_copies(pl.ds(i * BLOCK, BLOCK), i):
             cp.wait()
@@ -622,7 +932,10 @@
     narrow = (1,) + GRID + (ROWS, PAIR)
     links = []
     if linked:
-        outs = [jax.ShapeDtypeStruct(w.shape, F32) for w in rest]
+        outs = [
+            jax.ShapeDtypeStruct((PIECES, ROWS, CHUNK), F32),
+            jax.ShapeDtypeStruct((ROWS, PAIR), F32),
+        ]
         links += [pltpu.VMEM(wide, BF16), pltpu.VMEM(wide, BF16)]
         links += [pltpu.VMEM(narrow, BF16), pltpu.VMEM(narrow, BF16)]
         for n, _, _, _, _, r, lanes in (wide, narrow):
@@ -654,11 +967,12 @@
             pltpu.VMEM((slots, width), F32),
             pltpu.VMEM((8, ff), F32),
             pltpu.VMEM((8, ff), F32),
-            pltpu.VMEM((pairs, slots, 3 * PAIR), BF16),
+            pltpu.VMEM((pairs, slots, 2 * PAIR), BF16),
             pltpu.VMEM((pairs, PAIR, slots), BF16),
-            pltpu.VMEM((slots, width), BF16),
             pltpu.VMEM((pairs, PAIR, slots), BF16),
-            pltpu.VMEM((H, causal, BLOCK), BF16),
+            pltpu.VMEM((H, 1, slots), F32),
+            pltpu.VMEM((pairs, PAIR, slots), BF16),
+            pltpu.VMEM((H, BLOCK, causal), BF16),
             pltpu.VMEM((causal, BLOCK), F32),
             pltpu.VMEM((slots, ff), BF16),
             pltpu.VMEM((slots, ff), BF16),
@@ -672,6 +986,55 @@
         compiler_params=params,
         name="layer",
     )(lengths, x_in, y_in, grad_x, grad_y, *rest)
+
+
+def deliver_kernel(xo_hbm, yo_hbm, dx_hbm, shares, small, *refs):
+    streams, (d_qkv, d_out, d_up, d_down), vectors = refs[:3], refs[3:7], refs[7:12]
+    buffers, (load_sem, store_sem) = refs[12:15], refs[15:]
+    loads, stores = [], []
+    for k in range(4):
+        for n, (src, buf, dst) in enumerate(zip((xo_hbm, yo_hbm, dx_hbm), buffers, streams)):
+            part = pl.ds(k * (src.shape[0] // 4), src.shape[0] // 4)
+            loads.append(pltpu.make_async_copy(src.at[part], buf.at[part], load_sem.at[n, k]))
+            stores.append(pltpu.make_async_copy(buf.at[part], dst.at[part], store_sem.at[n, k]))
+    for cp in loads:
+        cp.start()
+    pairs, width = H // 2, d_out.shape[1]
+    for g in range(pairs):
+        for n in range(3):
+            lanes = slice(n * width + g * PAIR, n * width + (g + 1) * PAIR)
+            d_qkv[:, lanes] = shares[g, :, n * PAIR : (n + 1) * PAIR]
+        d_out[:, g * PAIR : (g + 1) * PAIR] = shares[g, :, 3 * PAIR :]
+    per = d_up.shape[1] // CHUNK
+    for j in range(per):
+        d_up[:, j * CHUNK : (j + 1) * CHUNK] = shares[pairs + j]
+        d_down[j * ROWS : (j + 1) * ROWS, :] = shares[pairs + per + j]
+    at = 0
+    for ref in vectors:
+        ref[...] = small[0, at : at + ref.shape[0]]
+        at += ref.shape[0]
+    for load, store in zip(loads, stores):
+        load.wait()
+        store.start()
+    for store in stores:
+        store.wait()
+
+
+def deliver(streams, shares, small, shapes):
+    vmem = pl.BlockSpec(memory_space=pltpu.VMEM)
+    any_ = pl.BlockSpec(memory_space=pl.ANY)
+    outs = [jax.ShapeDtypeStruct(s.shape, s.dtype) for s in streams]
+    outs += [jax.ShapeDtypeStruct(shape, F32) for shape in shapes]
+    return pl.pallas_call(
+        deliver_kernel,
+        out_shape=outs,
+        in_specs=[any_] * 3 + [vmem] * 2,
+        out_specs=[any_] * 3 + [vmem] * 9,
+        scratch_shapes=[pltpu.VMEM(s.shape, s.dtype) for s in streams]
+        + [pltpu.SemaphoreType.DMA((3, 4)), pltpu.SemaphoreType.DMA((3, 4))],
+        compiler_params=pltpu.CompilerParams(vmem_limit_bytes=VMEM_LIMIT),
+        name="deliver",
+    )(*streams, shares, small)
 
 
 BOTH = ("dp", "fsdp")
@@ -697,13 +1060,12 @@
     streams = (x_in, y_in, lengths, grad_x, grad_y)
     width = x_in.shape[1]
     if linked:
-        small = jnp.concatenate([gain_one, bias_one, gain_two, bias_two, b_up])
-        small = jnp.broadcast_to(small[None], (ROWS, small.shape[0]))
-        x_out, y_out, d_x, d_qkv, d_out, d_up, d_down, d_small = layer(
-            True, *streams, w_qkv, w_out, w_up, w_down, small
+        ends = (gain_one, bias_one, gain_two, bias_two, b_up)
+        *out_streams, shares, small = layer(True, *streams, w_qkv, w_out, w_up, w_down, *ends)
+        shapes = [w.shape for w in (w_qkv, w_out, w_up, w_down) + ends]
+        x_out, y_out, d_x, d_qkv, d_out, d_up, d_down, *vectors = deliver(
+            out_streams, shares, small, shapes
         )
-        row = d_small[0]
-        vectors = [row[n * ROWS : (n + 1) * ROWS] for n in range(4)] + [row[4 * ROWS :]]
     else:
         blocks = GRID[0] * GRID[1] * GRID[2] * GRID[3]
         pairs = H // 2

time: 171 us -> 119 us (0.70)
  Pallas kernels: 155 us -> 118 us
  local copies, waits for them, and re-layouts: 15.4 us -> 0 us
    pallas_call x1, Pallas kernels: 155 us -> 112 us  [layer(): pl.pallas_call(functools.partial(layer_kernel, linked), out_shape=streams...]
    unnamed x19 -> x0, local copies, waits for them, and re-layouts: 8.52 us -> none
    pallas_call x0 -> x1, Pallas kernels: none -> 6.66 us  [deliver(): pl.pallas_call(deliver_kernel, out_shape=outs, in_specs=[any_] * 3 + [vme...]
    concatenate x1 -> x0, local copies, waits for them, and re-layouts: 3.43 us -> none  [on_device(): small = jnp.concatenate([gain_one, bias_one, gain_two, bias_two, b_up])]
    slice x2 -> x0, local copies, waits for them, and re-layouts: 2.83 us -> none  [the longest x1 1.42 us: on_device(): row[n * ROWS:(n + 1) * ROWS]]
where the time goes in v2:
time: 119 us
  Pallas kernels  118 us (99%)
    pallas_call x1, Pallas kernels, layer(): pl.pallas_call(functools.partial(layer_kernel, linked), out_shape=streams...  112 us
    pallas_call x1, Pallas kernels, deliver(): pl.pallas_call(deliver_kernel, out_shape=outs, in_specs=[any_] * 3 + [vme...  6.66 us

profile of v2, /device:TPU:0, one launch (start us, length us, event | category | flops | bytes accessed | tf_op | source)
XLA Modules:
  0.0 119.1 jit_solution(8679450455005633715)
XLA Ops:
  0.6 111.6 %layer.1 = (bf16[1024,512]{1,0:T(8,128)(2,1)}, f32[1024,512]{1,0:T(8,128)}, f32[1024,512]{1,0:T(8,128)}, f32[12,16,512]{2,1,0:T(8,128)}, f32[16,128]{1,0:T(8,128)}) custom-call(s32[1,16]{1,0:T(1,128)} %refs_0_.1, bf16[1024,512]{1,0:T(8,128)(2,1)} %refs_1_.1, f32[1024,512]{1,0:T(8,128)} %refs_2_.1, bf16[1024,512]{1,0:T(8,128)(2,1)} %refs_3_.1, ...), custom_call_target="tpu_custom_call" | custom-call | tf_op jit(solution)/shard_map/layer/pallas_call | solution.py:956
  112.3 6.7 %deliver.1 = (bf16[1024,512]{1,0:T(8,128)(2,1)}, f32[1024,512]{1,0:T(8,128)}, f32[1024,512]{1,0:T(8,128)}, f32[16,1536]{1,0:T(8,128)}, f32[16,512]{1,0:T(8,128)}...) custom-call(bf16[1024,512]{1,0:T(8,128)(2,1)} %get-tuple-element.29., ...), custom_call_target="tpu_custom_call" | custom-call | tf_op jit(solution)/shard_map/deliver/pallas_call | solution.py:1028
